TPU v7x, 512 devices: a whole 4x4x16 slice. The times are simulated.
512 devices in a mesh: replica: 16 (over y, z_lo), fsdp: 32 (over x, z_hi, core).
Axes of the slice: x: 4, y: 4, z: 16 (z_hi: 4, z_lo: 4; z = z_hi * 4 + z_lo), core: 2. Of those that a mesh axis runs over, the one named last changes fastest.
Arguments:
- previous_global_weights: float32 [4194304], P('fsdp')
- replica_local_weights: float32 [16, 4194304], P('replica', 'fsdp')
- momentum: float32 [64, 4194304], P(None, ('fsdp', 'replica')), may hold values from -4 to 4
- reporting_replica_tokens: int32 [16], replicated, may hold values from 0 to 4096, as said below
- target_fragment_index: int32 [1], replicated, may hold values from 0 to 63
Outputs:
- new_weights: float32 [4194304], P('fsdp')
- new_momentum: float32 [4194304], P(('fsdp', 'replica'))
Inputs may be any that keep to these rules, and one draw needn't show every extreme that they name: `reporting_replica_tokens`: exactly one replica is lost and has 0 tokens; every other replica has 1024 or more.
All inputs are finite; a program needn't handle non-finite values.
Results may differ from a plain program's by a relative error of at most 0.000048.
Values sent between devices are 32-bit elements; how exact they have to be, the bound alone decides.
No kernel may reach another device: no remote copies, remote signals or barrier semaphores. Data moves between devices by JAX's collectives and lax.ppermute only.
A program may use at most 64 MiB of HBM per device.

v0:
```python
import math

import jax
import jax.numpy as jnp
from jax import lax
from jax.sharding import PartitionSpec as P

beta_outer = 0.9
rate_outer = 0.7
clip_scale = 2.0
epsilon = 1e-06


def local(
    previous_global_weights,
    replica_local_weights,
    momentum,
    reporting_replica_tokens,
    target_fragment_index,
):
    replicas = lax.axis_size("replica")
    replica_pos = lax.axis_index("replica")
    frag_total = previous_global_weights.shape[0] * lax.axis_size("fsdp")
    replica_token_weights = reporting_replica_tokens.astype(jnp.float32)
    reporting_count = jnp.sum(replica_token_weights)
    own_weight = lax.dynamic_index_in_dim(replica_token_weights, replica_pos, 0, keepdims=False)
    weighted = own_weight * (previous_global_weights - replica_local_weights[0])
    state_shard = lax.dynamic_index_in_dim(momentum, target_fragment_index[0], 0, keepdims=False)
    piece_len = previous_global_weights.shape[0] // replicas
    limit = clip_scale * math.sqrt(frag_total)
    masked_weight_total = lax.psum_scatter(weighted, "replica", scatter_dimension=0, tiled=True)
    mean_replica_weights = masked_weight_total / reporting_count
    squares = lax.psum(jnp.sum(mean_replica_weights * mean_replica_weights), ("replica", "fsdp"))
    grad_norm = jnp.sqrt(squares + epsilon)
    clipped = mean_replica_weights * jnp.minimum(1.0, limit / grad_norm)
    new_momentum = beta_outer * state_shard + clipped
    old_piece = lax.dynamic_slice_in_dim(
        previous_global_weights, replica_pos * piece_len, piece_len
    )
    new_piece = old_piece - rate_outer * (beta_outer * new_momentum + clipped)
    new_weights = lax.all_gather(new_piece, "replica", axis=0, tiled=True)
    return (new_weights, new_momentum)


def solution(mesh):
    placed = (P("fsdp"), P("replica", "fsdp"), P(None, ("fsdp", "replica")), P(), P())
    return jax.shard_map(
        local,
        mesh=mesh,
        in_specs=placed,
        out_specs=(P("fsdp"), P(("fsdp", "replica"))),
        check_vma=False,
    )
```

profile of v0, /device:TPU:2, one launch (start us, length us, event | category | flops | bytes accessed | tf_op | source)
XLA Modules:
  0.0 347.4 jit_solution(1930733209177733993)
XLA Ops:
  7.2 0.0 copy-start
  7.2 0.0 all-reduce.3.cloned.1.call-start
  7.2 0.7 convert_element_type.3
  7.9 0.6 dynamic_slice.13
  8.5 2.7 subtract_multiply_fusion
  11.2 0.0 all-reduce.3.cloned.1.call-update
  11.2 0.0 copy-done
  11.2 0.7 convert_reduce_fusion
  12.6 1.3 dynamic-slice
  14.5 1.0 dynamic-slice_multiply_fusion
  15.5 172.3 %all-reduce.3.cloned.1.call-done = f32[131072]{0:T(1024)} async-done(((f32[131072]{0:T(1024)}), f32[131072]{0:T(1024)}) %all-reduce.3.cloned.1.call-update) | async-done | bytes 524304
  187.8 2.1 multiply_reduce_fusion
  189.8 103.5 %psum.7 = f32[]{:T(128)} all-reduce(f32[]{:T(128)} %multiply_reduce_fusion), channel_id=1, replica_groups=mesh['replica'=16,'fsdp'=32] {'replica','fsdp'}, use_global_device_ids=true, to_apply=%region_3.4 | all-reduce | flops 1 | bytes 8 | tf_op jit(solution)/shard_map/psum | solution.py:33
  294.1 2.1 multiply_subtract_fusion
  296.2 43.5 %all_gather.3 = f32[131072]{0:T(1024)S(1)} all-gather(f32[8192]{0:T(1024)S(1)} %get-tuple-element.2), channel_id=1, replica_groups=mesh['replica'=16,'fsdp'=32] {'replica'}, dimensions={0}, use_global_device_ids=true | all-gather | bytes 557056 | tf_op jit(solution)/shard_map/all_gather | solution.py:41
  339.7 0.8 copy.10
Async XLA Ops:
  7.2 4.0 %copy-start = (s32[16]{0:T(128)S(1)}, s32[16]{0:T(128)}, u32[]{:S(2)}) copy-start(s32[16]{0:T(128)} %param.8) | copy-start | bytes 196
  7.2 180.6 %all-reduce.3.cloned.1.call-start = ((), (), s32[]{:S(2)}) async-start(), calls=%async_computation | async-start | bytes 1048576
Sparse Core Ops, SparseCore 0:
  11.5 176.2 all-reduce.2
where the time goes:
time: 348 us; the launch traced here: 347 us
  waiting for transfers between devices  172 us (49%)
  blocking collectives  147 us (42%)
  between operations  16.1 us (5%)
  other arithmetic  9.19 us (3%)
    unnamed x2, waiting for transfers between devices  172 us
    psum x1, blocking collectives, local(): lax.psum(jnp.sum(mean_replica_weights * mean_replica_weights), ('replica'...  104 us
    all_gather x1, blocking collectives, local(): new_weights = lax.all_gather(new_piece, 'replica', axis=0, tiled=True)  43.5 us
  transfers between devices with their start and end apart: 1, of which 1 were waited for; matrix products, arithmetic and copies ran while one was open for 1% of the time, Pallas kernels for 0%

commit v1 on v0

v1 whole, which is shorter than its diff:
```python
import math

import jax
import jax.numpy as jnp
from jax import lax
from jax.sharding import PartitionSpec as P

beta_outer = 0.9
rate_outer = 0.7
clip_scale = 2.0
epsilon = 1e-06
lanes = 128


def cross_groups(replicas, shards):
    def at(x, y, z, core):
        return (y * 4 + z % 4) * shards + x * 8 + (z // 4) * 2 + core

    planes = [
        [at(x, y, z, core) for x in range(4) for y in range(4)]
        for z in range(16)
        for core in range(2)
    ]
    columns = [
        [at(x, y, z, core) for z in range(16) for core in range(2)]
        for x in range(4)
        for y in range(4)
    ]
    return planes, columns


def group_sum(value, groups):
    spread = jnp.broadcast_to(value, (len(groups[0]), 1, lanes))
    parts = lax.all_to_all(
        spread, ("replica", "fsdp"), 0, 0, axis_index_groups=groups, tiled=True
    )
    return jnp.sum(parts[:, 0, 0])


def share(piece, count):
    spread = jnp.broadcast_to(piece[None], (count,) + piece.shape)
    return lax.all_to_all(spread, "replica", 0, 0, tiled=True)


def local(
    previous_global_weights,
    replica_local_weights,
    momentum,
    reporting_replica_tokens,
    target_fragment_index,
):
    replicas = lax.axis_size("replica")
    shards = lax.axis_size("fsdp")
    replica_pos = lax.axis_index("replica")
    frag_total = previous_global_weights.shape[0] * shards
    limit = clip_scale * math.sqrt(frag_total)
    token_weights = reporting_replica_tokens.astype(jnp.float32)
    reporting_count = jnp.sum(token_weights)
    blocks = previous_global_weights.reshape(replicas, -1, lanes)
    pieces = lax.all_to_all(
        replica_local_weights[0].reshape(blocks.shape), "replica", 0, 0, tiled=True
    )
    old_piece = lax.dynamic_index_in_dim(blocks, replica_pos, 0, keepdims=False)
    state = lax.dynamic_index_in_dim(momentum, target_fragment_index[0], 0, keepdims=False)
    state_piece = state.reshape(old_piece.shape)
    total = jnp.sum(token_weights[:, None, None] * (old_piece[None] - pieces), 0)
    average = total / reporting_count
    planes, columns = cross_groups(replicas, shards)
    squares = jnp.sum(average * average)
    squares = group_sum(squares, planes)
    squares = group_sum(squares, columns)
    all_state = share(state_piece, replicas)
    all_average = share(average, replicas)
    scale = jnp.minimum(1.0, limit / jnp.sqrt(squares + epsilon))
    new_momentum = beta_outer * state_piece + average * scale
    clipped = all_average * scale
    step = beta_outer * (beta_outer * all_state + clipped) + clipped
    new_weights = blocks - rate_outer * step
    return (new_weights.reshape(-1), new_momentum.reshape(-1))


def solution(mesh):
    placed = (P("fsdp"), P("replica", "fsdp"), P(None, ("fsdp", "replica")), P(), P())
    return jax.shard_map(
        local,
        mesh=mesh,
        in_specs=placed,
        out_specs=(P("fsdp"), P(("fsdp", "replica"))),
        check_vma=False,
    )
```

time: 348 us -> 108 us (0.31)
  the two profiles are of different devices: /device:TPU:2 before, /device:TPU:1 now
where the time goes in v1:
time: 108 us; the launch traced here: 107 us
  waiting for transfers between devices  45.9 us (42%)
  blocking collectives  26.5 us (25%)
  starting transfers between devices  21 us (19%)
  other arithmetic  7.1 us (7%)
  local copies, waits for them, and re-layouts  4.35 us (4%)
  between operations  2.03 us (2%)
    all_to_all x2, waiting for transfers between devices, share(): return lax.all_to_all(spread, 'replica', 0, 0, tiled=True)  28.2 us
    all_to_all x1, blocking collectives, group_sum(): lax.all_to_all(spread, ('replica', 'fsdp'), 0, 0, axis_index_groups=group...  26.5 us
    all_to_all x1, waiting for transfers between devices, local(): lax.all_to_all(replica_local_weights[0].reshape(blocks.shape), 'replica',...  12.4 us
    all_to_all x1, starting transfers between devices, local(): lax.all_to_all(replica_local_weights[0].reshape(blocks.shape), 'replica',...  9.2 us
    all_to_all x2, starting transfers between devices, share(): return lax.all_to_all(spread, 'replica', 0, 0, tiled=True)  7.42 us
    all_to_all x1, waiting for transfers between devices, group_sum(): lax.all_to_all(spread, ('replica', 'fsdp'), 0, 0, axis_index_groups=group...  5.33 us
    all_to_all x1, starting transfers between devices, group_sum(): lax.all_to_all(spread, ('replica', 'fsdp'), 0, 0, axis_index_groups=group...  4.43 us
  transfers between devices with their start and end apart: 4, of which 4 were waited for; matrix products, arithmetic and copies ran while one was open for 5% of the time, Pallas kernels for 0%

profile of v1, /device:TPU:1, one launch (start us, length us, event | category | flops | bytes accessed | tf_op | source)
XLA Modules:
  0.0 106.9 jit_solution(16297516802754421092)
XLA Ops:
  0.6 9.2 %all-to-all-start.1 = ((f32[16,64,128]{2,1,0:T(8,128)}), f32[16,64,128]{2,1,0:T(8,128)S(1)}, u32[]{:S(2)}, u32[]{:S(2)}) async-start(f32[16,64,128]{2,1,0:T(8,128)} %bitcast.16), calls=%async_computation.1 | async-start | bytes 1048576 | tf_op jit(solution)/shard_map/all_to_all | solution.py:60
  10.5 0.7 convert_element_type.3
  11.1 1.3 %convert_reduce_fusion = f32[]{:T(128)} fusion(s32[16]{0:T(128)} %param.8), kind=kLoop, calls=%fused_computation.10 | loop fusion | flops 31 | bytes 68 | tf_op jit(solution)/shard_map/reduce_sum | solution.py:58
  12.4 0.8 dynamic-slice_bitcast_fusion
  13.2 0.0 copy-start
  13.2 12.4 %all-to-all-done.1 = f32[16,64,128]{2,1,0:T(8,128)S(1)} async-done(((f32[16,64,128]{2,1,0:T(8,128)}), f32[16,64,128]{2,1,0:T(8,128)S(1)}, u32[]{:S(2)}, u32[]{:S(2)}) %all-to-all-start.1) | async-done | bytes 524320 | tf_op jit(solution)/shard_map/all_to_all | solution.py:60
  25.5 0.1 multiply_reduce_fusion
  25.7 1.3 %multiply_reduce_fusion.1 = (f32[]{:T(128)}, f32[64,128]{1,0:T(8,128)S(1)}) fusion(f32[64,128]{1,0:T(8,128)S(1)} %multiply_reduce_fusion, f32[]{:T(128)} %convert_reduce_fusion), kind=kLoop, calls=%fused_computation.3 | loop fusion | flops 24575 | bytes 65544 | tf_op jit(solution)/shard_map/reduce_sum | solution.py:69
  26.9 1.2 %broadcast_in_dim.24 = f32[16,1,128]{2,1,0:T(1,128)} broadcast(f32[]{:T(128)} %get-tuple-element.4), dimensions={} | broadcast | bytes 8196 | tf_op jit(solution)/shard_map/broadcast_in_dim | solution.py:33
  28.2 4.4 %all-to-all-start.3 = ((f32[16,1,128]{2,1,0:T(1,128)}), f32[16,1,128]{2,1,0:T(1,128)S(1)}, u32[]{:S(2)}, u32[]{:S(2)}) async-start(f32[16,1,128]{2,1,0:T(1,128)} %broadcast_in_dim.24), calls=%async_computation.3 | async-start | bytes 16384 | tf_op jit(solution)/shard_map/all_to_all | solution.py:34
  32.6 1.0 broadcast_multiply_fusion
  33.6 5.3 %all-to-all-done.3 = f32[16,1,128]{2,1,0:T(1,128)S(1)} async-done(((f32[16,1,128]{2,1,0:T(1,128)}), f32[16,1,128]{2,1,0:T(1,128)S(1)}, u32[]{:S(2)}, u32[]{:S(2)}) %all-to-all-start.3) | async-done | bytes 8224 | tf_op jit(solution)/shard_map/all_to_all | solution.py:34
  38.9 0.8 broadcast_in_dim.22
  39.8 3.8 %all-to-all-start = ((f32[16,64,128]{2,1,0:T(8,128)}), f32[16,64,128]{2,1,0:T(8,128)S(1)}, u32[]{:S(2)}, u32[]{:S(2)}) async-start(f32[16,64,128]{2,1,0:T(8,128)} %broadcast_in_dim.22), calls=%async_computation | async-start | bytes 1048576 | tf_op jit(solution)/shard_map/all_to_all | solution.py:42
  43.6 0.6 slice_reduce_fusion.1
  44.2 14.5 %all-to-all-done = f32[16,64,128]{2,1,0:T(8,128)S(1)} async-done(((f32[16,64,128]{2,1,0:T(8,128)}), f32[16,64,128]{2,1,0:T(8,128)S(1)}, u32[]{:S(2)}, u32[]{:S(2)}) %all-to-all-start) | async-done | bytes 524320 | tf_op jit(solution)/shard_map/all_to_all | solution.py:42
  58.8 0.7 broadcast_in_dim.25
  59.4 26.5 %all_to_all.25 = f32[32,1,128]{2,1,0:T(1,128)S(1)} all-to-all(f32[32,1,128]{2,1,0:T(1,128)S(1)} %broadcast_in_dim.25), channel_id=1, replica_groups={{0,1,32,33,64,65,96,97,2,3,34,35,66,67,98,99,4,5,36,37,68,69,100,101,6,..., dimensions={0} | all-to-all | bytes 32768 | tf_op jit(solution)/shard_map/all_to_all | solution.py:34
  85.9 0.8 broadcast_in_dim.23
  86.7 3.6 %all-to-all-start.2 = ((f32[16,64,128]{2,1,0:T(8,128)}), f32[16,64,128]{2,1,0:T(8,128)S(1)}, u32[]{:S(2)}, u32[]{:S(2)}) async-start(f32[16,64,128]{2,1,0:T(8,128)} %broadcast_in_dim.23), calls=%async_computation.2 | async-start | bytes 1048576 | tf_op jit(solution)/shard_map/all_to_all | solution.py:42
  90.3 0.6 slice_reduce_fusion
  91.6 0.6 bitcast_add_fusion
  92.3 13.7 %all-to-all-done.2 = f32[16,64,128]{2,1,0:T(8,128)S(1)} async-done(((f32[16,64,128]{2,1,0:T(8,128)}), f32[16,64,128]{2,1,0:T(8,128)S(1)}, u32[]{:S(2)}, u32[]{:S(2)}) %all-to-all-start.2) | async-done | bytes 524320 | tf_op jit(solution)/shard_map/all_to_all | solution.py:42
  106.0 0.0 copy-done
  106.0 0.9 multiply_subtract_fusion
Async XLA Ops:
  0.6 24.9 %all-to-all-start.1 = ((f32[16,64,128]{2,1,0:T(8,128)}), f32[16,64,128]{2,1,0:T(8,128)S(1)}, u32[]{:S(2)}, u32[]{:S(2)}) async-start(f32[16,64,128]{2,1,0:T(8,128)} %bitcast.16), calls=%async_computation.1 | async-start | bytes 1048576 | tf_op jit(solution)/shard_map/all_to_all | solution.py:60
  13.2 92.8 %copy-start = (f32[131072]{0:T(1024)S(1)}, f32[131072]{0:T(1024)}, u32[]{:S(2)}) copy-start(f32[131072]{0:T(1024)} %param.5) | copy-start | bytes 1572868
  28.2 10.8 %all-to-all-start.3 = ((f32[16,1,128]{2,1,0:T(1,128)}), f32[16,1,128]{2,1,0:T(1,128)S(1)}, u32[]{:S(2)}, u32[]{:S(2)}) async-start(f32[16,1,128]{2,1,0:T(1,128)} %broadcast_in_dim.24), calls=%async_computation.3 | async-start | bytes 16384 | tf_op jit(solution)/shard_map/all_to_all | solution.py:34
  39.8 19.0 %all-to-all-start = ((f32[16,64,128]{2,1,0:T(8,128)}), f32[16,64,128]{2,1,0:T(8,128)S(1)}, u32[]{:S(2)}, u32[]{:S(2)}) async-start(f32[16,64,128]{2,1,0:T(8,128)} %broadcast_in_dim.22), calls=%async_computation | async-start | bytes 1048576 | tf_op jit(solution)/shard_map/all_to_all | solution.py:42
  86.7 19.3 %all-to-all-start.2 = ((f32[16,64,128]{2,1,0:T(8,128)}), f32[16,64,128]{2,1,0:T(8,128)S(1)}, u32[]{:S(2)}, u32[]{:S(2)}) async-start(f32[16,64,128]{2,1,0:T(8,128)} %broadcast_in_dim.23), calls=%async_computation.2 | async-start | bytes 1048576 | tf_op jit(solution)/shard_map/all_to_all | solution.py:42

commit v2 on v0

v2 whole, which is shorter than its diff:
```python
import math

import jax
import jax.numpy as jnp
from jax import lax
from jax.sharding import PartitionSpec as P

beta_outer = 0.9
rate_outer = 0.7
clip_scale = 2.0
epsilon = 1e-06
lanes = 128


def line_groups(replicas):
    along_y = [[y * 4 + z for y in range(4)] for z in range(4)]
    along_z = [[y * 4 + z for z in range(4)] for y in range(4)]
    return along_y, along_z


def local(
    previous_global_weights,
    replica_local_weights,
    momentum,
    reporting_replica_tokens,
    target_fragment_index,
):
    replicas = lax.axis_size("replica")
    shards = lax.axis_size("fsdp")
    replica_pos = lax.axis_index("replica")
    row, column = replica_pos // 4, replica_pos % 4
    frag_total = previous_global_weights.shape[0] * shards
    limit = clip_scale * math.sqrt(frag_total)
    along_y, along_z = line_groups(replicas)
    token_weights = reporting_replica_tokens.astype(jnp.float32)
    reporting_count = jnp.sum(token_weights)
    blocks = previous_global_weights.reshape(4, -1, lanes)
    depth = blocks.shape[1]
    old_block = lax.dynamic_index_in_dim(blocks, row, 0, keepdims=False)
    state = lax.dynamic_index_in_dim(momentum, target_fragment_index[0], 0, keepdims=False)
    state_piece = state.reshape(-1, lanes)
    column_weights = lax.dynamic_index_in_dim(token_weights.reshape(4, 4), column, 1, keepdims=False)
    received = lax.all_to_all(
        replica_local_weights[0].reshape(blocks.shape), "replica", 0, 0, axis_index_groups=along_y, tiled=True
    )
    partial = jnp.sum(column_weights[:, None, None] * (old_block[None] - received), 0)

    sent = jnp.concatenate([partial, state_piece], 0)
    parts = lax.all_gather(sent, "replica", axis=0, axis_index_groups=along_z)
    average = jnp.sum(parts[:, :depth], 0) / reporting_count
    state_block = parts[:, depth:].reshape(depth, lanes)
    squares = jnp.broadcast_to(jnp.sum(average * average), (8, lanes))
    sent = jnp.concatenate([average, state_block, squares], 0)
    sent = jnp.broadcast_to(sent[None], (4,) + sent.shape)
    parts = lax.all_to_all(sent, "replica", 0, 0, axis_index_groups=along_y, tiled=True)
    squares = jnp.sum(parts[:, 2 * depth, 0])
    parts_f = lax.all_to_all(jnp.broadcast_to(squares, (shards, 1, lanes)), "fsdp", 0, 0, tiled=True)
    squares = jnp.sum(parts_f[:, 0, 0])
    scale = jnp.minimum(1.0, limit / jnp.sqrt(squares + epsilon))
    own = lax.dynamic_slice_in_dim(average, column * (depth // 4), depth // 4, 0)
    new_momentum = beta_outer * state_piece + own * scale
    clipped = parts[:, :depth] * scale
    step = beta_outer * (beta_outer * parts[:, depth : 2 * depth] + clipped) + clipped
    new_weights = blocks - rate_outer * step
    return (new_weights.reshape(-1), new_momentum.reshape(-1))


def solution(mesh):
    placed = (P("fsdp"), P("replica", "fsdp"), P(None, ("fsdp", "replica")), P(), P())
    return jax.shard_map(
        local,
        mesh=mesh,
        in_specs=placed,
        out_specs=(P("fsdp"), P(("fsdp", "replica"))),
        check_vma=False,
    )
```

time: 348 us -> 87.1 us (0.25)
  the two profiles are of different devices: /device:TPU:2 before, /device:TPU:1 now
where the time goes in v2:
time: 87.1 us; the launch traced here: 86.8 us
  blocking collectives  29.9 us (34%)
  starting transfers between devices  27.1 us (31%)
  waiting for transfers between devices  18.5 us (21%)
  other arithmetic  6 us (7%)
  local copies, waits for them, and re-layouts  3.22 us (4%)
  between operations  2.13 us (2%)
    all_to_all x1, starting transfers between devices, local(): lax.all_to_all(jnp.broadcast_to(squares, (shards, 1, lanes)), 'fsdp', 0,...  21.9 us
    all_gather x1, blocking collectives, local(): parts = lax.all_gather(sent, 'replica', axis=0, axis_index_groups=along_z)  17.7 us
    all_to_all x1, waiting for transfers between devices, local(): lax.all_to_all(jnp.broadcast_to(squares, (shards, 1, lanes)), 'fsdp', 0,...  14.1 us
    all_to_all x1, blocking collectives, local(): lax.all_to_all(sent, 'replica', 0, 0, axis_index_groups=along_y, tiled=True)  12.2 us
    all_to_all x1, starting transfers between devices, local(): lax.all_to_all(replica_local_weights[0].reshape(blocks.shape), 'replica',...  5.16 us
    all_to_all x1, waiting for transfers between devices, local(): lax.all_to_all(replica_local_weights[0].reshape(blocks.shape), 'replica',...  4.39 us
    sub x1, other arithmetic, local(): new_weights = blocks - rate_outer * step  1.96 us
  transfers between devices with their start and end apart: 2, of which 2 were waited for; matrix products, arithmetic and copies ran while one was open for 2% of the time, Pallas kernels for 0%

profile of v2, /device:TPU:1, one launch (start us, length us, event | category | flops | bytes accessed | tf_op | source)
XLA Modules:
  0.0 86.8 jit_solution(6687892862242750538)
XLA Ops:
  0.6 0.0 copy-start
  0.6 0.0 copy-start.1
  0.7 5.2 %all-to-all-start = ((f32[4,256,128]{2,1,0:T(8,128)}), f32[4,256,128]{2,1,0:T(8,128)S(1)}, u32[]{:S(2)}, u32[]{:S(2)}) async-start(f32[4,256,128]{2,1,0:T(8,128)} %bitcast.19), calls=%async_computation | async-start | bytes 1048576 | tf_op jit(solution)/shard_map/all_to_all | solution.py:43
  6.5 0.0 copy-done
  6.5 0.0 copy-done.1
  6.6 0.1 reshape.27
  6.6 0.2 dynamic-slice_reduce_fusion
  6.8 0.6 convert_reduce_fusion
  7.4 0.9 %dynamic-slice_bitcast_fusion = f32[256,128]{1,0:T(8,128)S(1)} fusion(f32[4,256,128]{2,1,0:T(8,128)} %bitcast.16, s32[]{:T(128)S(6)} %select_n.29), kind=kLoop, calls=%fused_computation.12 | loop fusion | bytes 262148 | tf_op jit(solution)/shard_map/sub | solution.py:46
  8.4 4.4 %all-to-all-done = f32[4,256,128]{2,1,0:T(8,128)S(1)} async-done(((f32[4,256,128]{2,1,0:T(8,128)}), f32[4,256,128]{2,1,0:T(8,128)S(1)}, u32[]{:S(2)}, u32[]{:S(2)}) %all-to-all-start) | async-done | bytes 524320 | tf_op jit(solution)/shard_map/all_to_all | solution.py:43
  12.7 0.1 multiply_reduce_fusion
  12.9 17.7 %all-gather = f32[1280,128]{1,0:T(8,128)S(1)} all-gather(f32[320,128]{1,0:T(8,128)S(1)} %pad_maximum_fusion), channel_id=2, replica_groups={{0,32,64,96},{128,160,192,224},{256,288,320,352},{384,416,448,480},{1,3..., dimensions={0}, use_global_device_ids=true | all-gather | bytes 819200 | tf_op jit(solution)/shard_map/all_gather | solution.py:49
  30.6 1.3 %multiply_reduce_fusion.1 = (f32[]{:T(128)}, f32[256,128]{1,0:T(8,128)S(1)}) fusion(f32[256,128]{1,0:T(8,128)S(1)} %slice_reduce_fusion, f32[]{:T(128)} %convert_reduce_fusion), kind=kLoop, calls=%fused_computation.11 | loop fusion | flops 98303 | bytes 262152 | tf_op jit(solution)/shard_map/reduce_sum | solution.py:52
  31.9 0.6 broadcast_in_dim.6
  32.5 0.1 maximum_maximum_fusion
  32.7 0.1 broadcast_in_dim.7
  32.8 12.2 %all_to_all.15 = f32[4,520,128]{2,1,0:T(8,128)S(1)} all-to-all(f32[4,520,128]{2,1,0:T(8,128)S(1)} %broadcast_in_dim.7), channel_id=1, replica_groups={{0,128,256,384},{32,160,288,416},{64,192,320,448},{96,224,352,480},{1,1..., dimensions={0} | all-to-all | bytes 2129920 | tf_op jit(solution)/shard_map/all_to_all | solution.py:55
  45.0 0.6 slice_reduce_fusion.2
  45.6 1.3 %broadcast_in_dim.16 = f32[32,1,128]{2,1,0:T(1,128)} broadcast(f32[]{:T(128)} %slice_reduce_fusion.2), dimensions={} | broadcast | bytes 16388 | tf_op jit(solution)/shard_map/broadcast_in_dim | solution.py:57
  46.8 21.9 %all-to-all-start.2 = ((f32[32,1,128]{2,1,0:T(1,128)}), f32[32,1,128]{2,1,0:T(1,128)S(1)}, u32[]{:S(2)}, u32[]{:S(2)}) async-start(f32[32,1,128]{2,1,0:T(1,128)} %broadcast_in_dim.16), calls=%async_computation.2 | async-start | bytes 32768 | tf_op jit(solution)/shard_map/all_to_all | solution.py:57
  68.8 14.1 %all-to-all-done.2 = f32[32,1,128]{2,1,0:T(1,128)S(1)} async-done(((f32[32,1,128]{2,1,0:T(1,128)}), f32[32,1,128]{2,1,0:T(1,128)S(1)}, u32[]{:S(2)}, u32[]{:S(2)}) %all-to-all-start.2) | async-done | bytes 16416 | tf_op jit(solution)/shard_map/all_to_all | solution.py:57
  82.9 0.6 slice_reduce_fusion.1
  84.2 0.6 add_bitcast_fusion
  84.8 2.0 %fusion.4 = f32[4,256,128]{2,1,0:T(8,128)} fusion(f32[4,256,128]{2,1,0:T(8,128)} %bitcast.17, f32[4,520,128]{2,1,0:T(8,128)S(1)} %all_to_all.15, f32[]{:T(128)S(6)} %min_shard_map.3), kind=kLoop, calls=%fused_computation.6 | loop fusion | flops 917504 | bytes 2097156 | tf_op jit(solution)/shard_map/sub | solution.py:64
  (6 shorter events, 0.1 us)
Async XLA Ops:
  0.6 5.8 %copy-start = (f32[64,8192]{1,0:T(8,128)S(1)}, f32[64,8192]{1,0:T(8,128)}, u32[]{:S(2)}) copy-start(f32[64,8192]{1,0:T(8,128)} %param.7) | copy-start | bytes 6291460
  0.6 5.9 %copy-start.1 = (s32[16]{0:T(128)S(1)}, s32[16]{0:T(128)}, u32[]{:S(2)}) copy-start(s32[16]{0:T(128)} %param.8) | copy-start | bytes 196
  0.7 12.1 %all-to-all-start = ((f32[4,256,128]{2,1,0:T(8,128)}), f32[4,256,128]{2,1,0:T(8,128)S(1)}, u32[]{:S(2)}, u32[]{:S(2)}) async-start(f32[4,256,128]{2,1,0:T(8,128)} %bitcast.19), calls=%async_computation | async-start | bytes 1048576 | tf_op jit(solution)/shard_map/all_to_all | solution.py:43
  46.8 36.0 %all-to-all-start.2 = ((f32[32,1,128]{2,1,0:T(1,128)}), f32[32,1,128]{2,1,0:T(1,128)S(1)}, u32[]{:S(2)}, u32[]{:S(2)}) async-start(f32[32,1,128]{2,1,0:T(1,128)} %broadcast_in_dim.16), calls=%async_computation.2 | async-start | bytes 32768 | tf_op jit(solution)/shard_map/all_to_all | solution.py:57

commit v3 on v2

--- a/solution.py
+++ b/solution.py
@@ -10,6 +10,16 @@
 clip_scale = 2.0
 epsilon = 1e-06
 lanes = 128
+
+
+def scalar_groups(shards):
+    near = [
+        [(y * 4 + z) * shards + x * 8 + far * 2 + core for y in range(4) for x in range(4) for core in range(2)]
+        for z in range(4)
+        for far in range(4)
+    ]
+    far = [[x * 8 + z * 2 + core for z in range(4)] for x in range(4) for core in range(2)]
+    return near, far
 
 
 def line_groups(replicas):
@@ -49,13 +59,15 @@
     parts = lax.all_gather(sent, "replica", axis=0, axis_index_groups=along_z)
     average = jnp.sum(parts[:, :depth], 0) / reporting_count
     state_block = parts[:, depth:].reshape(depth, lanes)
-    squares = jnp.broadcast_to(jnp.sum(average * average), (8, lanes))
-    sent = jnp.concatenate([average, state_block, squares], 0)
+    near, far = scalar_groups(shards)
+    squares = jnp.broadcast_to(jnp.sum(average * average), (len(near[0]), 1, lanes))
+    squares = lax.all_to_all(squares, ("replica", "fsdp"), 0, 0, axis_index_groups=near, tiled=True)
+    squares = jnp.sum(squares[:, 0, 0])
+    sent = jnp.concatenate([average, state_block], 0)
+    sent, squares = lax.optimization_barrier((sent, squares))
     sent = jnp.broadcast_to(sent[None], (4,) + sent.shape)
     parts = lax.all_to_all(sent, "replica", 0, 0, axis_index_groups=along_y, tiled=True)
-    squares = jnp.sum(parts[:, 2 * depth, 0])
-    parts_f = lax.all_to_all(jnp.broadcast_to(squares, (shards, 1, lanes)), "fsdp", 0, 0, tiled=True)
-    squares = jnp.sum(parts_f[:, 0, 0])
+    squares = lax.psum(squares, "fsdp", axis_index_groups=far)
     scale = jnp.minimum(1.0, limit / jnp.sqrt(squares + epsilon))
     own = lax.dynamic_slice_in_dim(average, column * (depth // 4), depth // 4, 0)
     new_momentum = beta_outer * state_piece + own * scale

time: 87.1 us -> 78 us (0.90)
  the two profiles are of different devices: /device:TPU:1 before, /device:TPU:8 now
where the time goes in v3:
time: 78 us; the launch traced here: 77.6 us
  blocking collectives  37.2 us (48%)
  starting transfers between devices  19.3 us (25%)
  waiting for transfers between devices  8.93 us (11%)
  other arithmetic  6.6 us (8%)
  local copies, waits for them, and re-layouts  3.55 us (5%)
  between operations  2.08 us (3%)
    psum x1, blocking collectives, local(): squares = lax.psum(squares, 'fsdp', axis_index_groups=far)  20.6 us
    all_gather x1, blocking collectives, local(): parts = lax.all_gather(sent, 'replica', axis=0, axis_index_groups=along_z)  16.5 us
    all_to_all x1, starting transfers between devices, local(): lax.all_to_all(replica_local_weights[0].reshape(blocks.shape), 'replica',...  9.4 us
    all_to_all x1, waiting for transfers between devices, local(): lax.all_to_all(squares, ('replica', 'fsdp'), 0, 0, axis_index_groups=near...  6.14 us
    all_to_all x1, starting transfers between devices, local(): lax.all_to_all(squares, ('replica', 'fsdp'), 0, 0, axis_index_groups=near...  4.99 us
    all_to_all x1, starting transfers between devices, local(): lax.all_to_all(sent, 'replica', 0, 0, axis_index_groups=along_y, tiled=True)  4.89 us
    all_to_all x1, waiting for transfers between devices, local(): lax.all_to_all(replica_local_weights[0].reshape(blocks.shape), 'replica',...  2.78 us
    sub x1, other arithmetic, local(): new_weights = blocks - rate_outer * step  1.96 us
  transfers between devices with their start and end apart: 3, of which 2 were waited for; matrix products, arithmetic and copies ran while one was open for 5% of the time, Pallas kernels for 0%

profile of v3, /device:TPU:8, one launch (start us, length us, event | category | flops | bytes accessed | tf_op | source)
XLA Modules:
  0.0 77.6 jit_solution(15718431624247113925)
XLA Ops:
  0.6 0.0 copy-start
  0.6 9.4 %all-to-all-start = ((f32[4,256,128]{2,1,0:T(8,128)}), f32[4,256,128]{2,1,0:T(8,128)S(1)}, u32[]{:S(2)}, u32[]{:S(2)}) async-start(f32[4,256,128]{2,1,0:T(8,128)} %bitcast.19), calls=%async_computation | async-start | bytes 1048576 | tf_op jit(solution)/shard_map/all_to_all | solution.py:53
  10.7 0.0 copy-done
  10.8 0.7 convert_element_type.3
  11.4 0.1 reshape.27
  11.5 0.2 dynamic-slice_reduce_fusion
  11.7 1.3 %convert_reduce_fusion = f32[]{:T(128)} fusion(s32[16]{0:T(128)} %param.8), kind=kLoop, calls=%fused_computation.18 | loop fusion | flops 31 | bytes 68 | tf_op jit(solution)/shard_map/reduce_sum | solution.py:46
  13.0 0.9 %dynamic-slice_bitcast_fusion = f32[256,128]{1,0:T(8,128)S(1)} fusion(f32[4,256,128]{2,1,0:T(8,128)} %bitcast.16, s32[]{:T(128)S(6)} %select_n.29), kind=kLoop, calls=%fused_computation.12 | loop fusion | bytes 262148 | tf_op jit(solution)/shard_map/sub | solution.py:56
  13.9 2.8 %all-to-all-done = f32[4,256,128]{2,1,0:T(8,128)S(1)} async-done(((f32[4,256,128]{2,1,0:T(8,128)}), f32[4,256,128]{2,1,0:T(8,128)S(1)}, u32[]{:S(2)}, u32[]{:S(2)}) %all-to-all-start) | async-done | bytes 524320 | tf_op jit(solution)/shard_map/all_to_all | solution.py:53
  16.7 0.1 multiply_reduce_fusion
  16.8 16.5 %all-gather = f32[1280,128]{1,0:T(8,128)S(1)} all-gather(f32[320,128]{1,0:T(8,128)S(1)} %pad_maximum_fusion.1), channel_id=2, replica_groups={{0,32,64,96},{128,160,192,224},{256,288,320,352},{384,416,448,480},{1,3..., dimensions={0}, use_global_device_ids=true | all-gather | bytes 819200 | tf_op jit(solution)/shard_map/all_gather | solution.py:59
  33.4 1.3 %multiply_reduce_fusion.1 = (f32[]{:T(128)}, f32[256,128]{1,0:T(8,128)S(1)}) fusion(f32[256,128]{1,0:T(8,128)S(1)} %slice_reduce_fusion, f32[]{:T(128)} %convert_reduce_fusion), kind=kLoop, calls=%fused_computation.11 | loop fusion | flops 98303 | bytes 262152 | tf_op jit(solution)/shard_map/reduce_sum | solution.py:63
  34.7 1.3 %broadcast_in_dim.4 = f32[32,1,128]{2,1,0:T(1,128)} broadcast(f32[]{:T(128)} %get-tuple-element.6), dimensions={} | broadcast | bytes 16388 | tf_op jit(solution)/shard_map/broadcast_in_dim | solution.py:63
  36.0 5.0 %all-to-all-start.1 = ((f32[32,1,128]{2,1,0:T(1,128)}), f32[32,1,128]{2,1,0:T(1,128)S(1)}, u32[]{:S(2)}, u32[]{:S(2)}) async-start(f32[32,1,128]{2,1,0:T(1,128)} %broadcast_in_dim.4), calls=%async_computation.1 | async-start | bytes 32768 | tf_op jit(solution)/shard_map/all_to_all | solution.py:64
  41.0 6.1 %all-to-all-done.1 = f32[32,1,128]{2,1,0:T(1,128)S(1)} async-done(((f32[32,1,128]{2,1,0:T(1,128)}), f32[32,1,128]{2,1,0:T(1,128)S(1)}, u32[]{:S(2)}, u32[]{:S(2)}) %all-to-all-start.1) | async-done | bytes 16416 | tf_op jit(solution)/shard_map/all_to_all | solution.py:64
  47.1 0.6 slice_reduce_fusion.1
  47.8 1.1 %broadcast_in_dim.5 = f32[4,512,128]{2,1,0:T(8,128)} broadcast(f32[512,128]{1,0:T(8,128)S(1)} %pad_maximum_fusion), dimensions={1,2} | broadcast | bytes 1310720 | tf_op jit(solution)/shard_map/broadcast_in_dim | solution.py:68
  48.8 4.9 %all-to-all-start.2 = ((f32[4,512,128]{2,1,0:T(8,128)}), f32[4,512,128]{2,1,0:T(8,128)S(1)}, u32[]{:S(2)}, u32[]{:S(2)}) async-start(f32[4,512,128]{2,1,0:T(8,128)} %broadcast_in_dim.5), calls=%async_computation.2 | async-start | bytes 2097152 | tf_op jit(solution)/shard_map/all_to_all | solution.py:69
  53.7 20.6 %psum.7 = f32[]{:T(128)} all-reduce(f32[]{:T(128)} %slice_reduce_fusion.1), channel_id=1, replica_groups={{0,2,4,6},{1,3,5,7},{8,10,12,14},{9,11,13,15},{16,18,20,22},{17,19,21,2..., use_global_device_ids=true, to_apply=%region_5.6 | all-reduce | flops 1 | bytes 8 | tf_op jit(solution)/shard_map/psum | solution.py:70
  75.0 0.6 add_bitcast_fusion
  75.7 0.0 all-to-all-done.2
  75.7 2.0 %fusion.4 = f32[4,256,128]{2,1,0:T(8,128)} fusion(f32[4,256,128]{2,1,0:T(8,128)} %bitcast.17, f32[4,512,128]{2,1,0:T(8,128)S(1)} %all-to-all-done.2, f32[]{:T(128)S(6)} %min_shard_map.3), kind=kLoop, calls=%fused_computation.6 | loop fusion | flops 917504 | bytes 2097156 | tf_op jit(solution)/shard_map/sub | solution.py:76
  (5 shorter events, 0.1 us)
Async XLA Ops:
  0.6 10.1 %copy-start = (f32[64,8192]{1,0:T(8,128)S(1)}, f32[64,8192]{1,0:T(8,128)}, u32[]{:S(2)}) copy-start(f32[64,8192]{1,0:T(8,128)} %param.7) | copy-start | bytes 6291460
  0.6 16.0 %all-to-all-start = ((f32[4,256,128]{2,1,0:T(8,128)}), f32[4,256,128]{2,1,0:T(8,128)S(1)}, u32[]{:S(2)}, u32[]{:S(2)}) async-start(f32[4,256,128]{2,1,0:T(8,128)} %bitcast.19), calls=%async_computation | async-start | bytes 1048576 | tf_op jit(solution)/shard_map/all_to_all | solution.py:53
  36.0 11.2 %all-to-all-start.1 = ((f32[32,1,128]{2,1,0:T(1,128)}), f32[32,1,128]{2,1,0:T(1,128)S(1)}, u32[]{:S(2)}, u32[]{:S(2)}) async-start(f32[32,1,128]{2,1,0:T(1,128)} %broadcast_in_dim.4), calls=%async_computation.1 | async-start | bytes 32768 | tf_op jit(solution)/shard_map/all_to_all | solution.py:64
  48.8 26.8 %all-to-all-start.2 = ((f32[4,512,128]{2,1,0:T(8,128)}), f32[4,512,128]{2,1,0:T(8,128)S(1)}, u32[]{:S(2)}, u32[]{:S(2)}) async-start(f32[4,512,128]{2,1,0:T(8,128)} %broadcast_in_dim.5), calls=%async_computation.2 | async-start | bytes 2097152 | tf_op jit(solution)/shard_map/all_to_all | solution.py:69

commit v4 on v3

v4 whole, which is shorter than its diff:
```python
import math

import jax
import jax.numpy as jnp
from jax import lax
from jax.sharding import PartitionSpec as P

beta_outer = 0.9
rate_outer = 0.7
clip_scale = 2.0
epsilon = 1e-06
lanes = 128


def block_groups():
    return [[y * 4 + half * 2 + side for y in range(4) for side in range(2)] for half in range(2)]


def line_groups():
    return [[y * 4 + z for y in range(4)] for z in range(4)]


def near_groups(shards):
    return [
        [
            (y * 4 + half * 2 + side) * shards + x * 8 + far * 2 + core
            for y in range(4)
            for side in range(2)
            for x in range(4)
            for core in range(2)
        ]
        for half in range(2)
        for far in range(4)
    ]


def far_groups():
    return [[x * 8 + far * 2 + core for far in range(4)] for x in range(4) for core in range(2)]


def local(
    previous_global_weights,
    replica_local_weights,
    momentum,
    reporting_replica_tokens,
    target_fragment_index,
):
    replicas = lax.axis_size("replica")
    shards = lax.axis_size("fsdp")
    replica_pos = lax.axis_index("replica")
    row, half, side = replica_pos >> 2, (replica_pos >> 1) & 1, replica_pos & 1
    frag_total = previous_global_weights.shape[0] * shards
    limit = clip_scale * math.sqrt(frag_total)
    token_weights = reporting_replica_tokens.astype(jnp.float32)
    reporting_count = jnp.sum(token_weights)
    blocks = previous_global_weights.reshape(8, -1, lanes)
    depth = blocks.shape[1]
    old_block = lax.dynamic_index_in_dim(blocks, row * 2 + side, 0, keepdims=False)
    state = lax.dynamic_index_in_dim(momentum, target_fragment_index[0], 0, keepdims=False)
    state_piece = state.reshape(-1, lanes)
    group_weights = lax.dynamic_index_in_dim(
        token_weights.reshape(4, 2, 2), half, 1, keepdims=False
    ).reshape(8)
    received = lax.all_to_all(
        replica_local_weights[0].reshape(blocks.shape),
        "replica", 0, 0, axis_index_groups=block_groups(), tiled=True,
    )
    partial = jnp.sum(group_weights[:, None, None] * (old_block[None] - received), 0)
    sent = jnp.concatenate([partial, state_piece], 0)
    other = lax.ppermute(sent, "replica", [(i, i ^ 2) for i in range(replicas)])
    average = (partial + other[:depth]) / reporting_count
    pair = jnp.stack([state_piece, other[depth:]])
    pair = jnp.where(half == 0, pair, pair[::-1]).reshape(depth, lanes)
    near = near_groups(shards)
    squares = jnp.broadcast_to(jnp.sum(average * average), (len(near[0]), 1, lanes))
    mine = jnp.concatenate([average, pair], 0)
    beside = lax.ppermute(mine, "replica", [(i, i ^ 1) for i in range(replicas)])
    squares = lax.all_to_all(squares, ("replica", "fsdp"), 0, 0, axis_index_groups=near, tiled=True)
    squares = jnp.sum(squares[:, 0, 0])
    sent = jnp.where(side == 0, jnp.stack([mine, beside]), jnp.stack([beside, mine]))
    sent, squares = lax.optimization_barrier((sent, squares))
    sent = jnp.broadcast_to(sent[None], (4,) + sent.shape)
    parts = lax.all_to_all(sent, "replica", 0, 0, axis_index_groups=line_groups(), tiled=True)
    parts = parts.reshape(8, -1, lanes)
    squares = lax.psum(squares, "fsdp", axis_index_groups=far_groups())
    scale = jnp.minimum(1.0, limit / jnp.sqrt(squares + epsilon))
    pieces = parts[:, :depth].reshape(replicas, -1, lanes)
    own = lax.dynamic_index_in_dim(pieces, replica_pos, 0, keepdims=False)
    new_momentum = beta_outer * state_piece + own * scale
    clipped = pieces * scale
    all_state = parts[:, depth:].reshape(4, 2, 2, -1, lanes).swapaxes(1, 2).reshape(pieces.shape)
    step = beta_outer * (beta_outer * all_state + clipped) + clipped
    new_weights = blocks.reshape(pieces.shape) - rate_outer * step
    return (new_weights.reshape(-1), new_momentum.reshape(-1))


def solution(mesh):
    placed = (P("fsdp"), P("replica", "fsdp"), P(None, ("fsdp", "replica")), P(), P())
    return jax.shard_map(
        local,
        mesh=mesh,
        in_specs=placed,
        out_specs=(P("fsdp"), P(("fsdp", "replica"))),
        check_vma=False,
    )
```

time: 78 us -> 70.8 us (0.908)
  blocking collectives: 37.2 us -> 20.4 us
  starting transfers between devices: 19.3 us -> 26.9 us
  waiting for transfers between devices: 8.93 us -> 11.4 us
    all_gather x1 -> x0, blocking collectives: 16.5 us -> none  [local(): parts = lax.all_gather(sent, 'replica', axis=0, axis_index_groups=along_z)]
    ppermute x0 -> x2, starting transfers between devices: none -> 6.83 us  [the longest x1 3.43 us: local(): lax.ppermute(mine, 'replica', [(i, i ^ 1) for i in range(replicas)])]
    ppermute x0 -> x2, waiting for transfers between devices: none -> 4.44 us  [the longest x1 4.44 us: local(): other = lax.ppermute(sent, 'replica', [(i, i ^ 2) for i in range(replicas)])]
    all_to_all x1, waiting for transfers between devices: 6.14 us -> 3.47 us  [local(): lax.all_to_all(squares, ('replica', 'fsdp'), 0, 0, axis_index_groups=near...]
    sub x1, other arithmetic: 1.96 us -> 0.89 us  [local(): new_weights = blocks.reshape(pieces.shape) - rate_outer * step]
    all_to_all x1, starting transfers between devices: 4.99 us -> 6 us  [local(): lax.all_to_all(squares, ('replica', 'fsdp'), 0, 0, axis_index_groups=near...]
    mul x0 -> x1, other arithmetic: none -> 1 us  [local(): new_momentum = beta_outer * state_piece + own * scale]
  transfers between devices with their start and end apart: 3 -> 5, of which waited for: 2 -> 3; matrix products, arithmetic and copies ran while one was open for 5% -> 6% of each run, Pallas kernels for 0% -> 0%
where the time goes in v4:
time: 70.8 us; the launch traced here: 70.3 us
  starting transfers between devices  26.9 us (38%)
  blocking collectives  20.4 us (29%)
  waiting for transfers between devices  11.4 us (16%)
  other arithmetic  6.04 us (9%)
  local copies, waits for them, and re-layouts  3.43 us (5%)
  between operations  2.12 us (3%)
    psum x1, blocking collectives, local(): squares = lax.psum(squares, 'fsdp', axis_index_groups=far_groups())  20.4 us
    all_to_all x1, starting transfers between devices, local(): lax.all_to_all(replica_local_weights[0].reshape(blocks.shape), 'replica',...  9.24 us
    all_to_all x1, starting transfers between devices, local(): lax.all_to_all(squares, ('replica', 'fsdp'), 0, 0, axis_index_groups=near...  6 us
    all_to_all x1, starting transfers between devices, local(): lax.all_to_all(sent, 'replica', 0, 0, axis_index_groups=line_groups(), ti...  4.88 us
    ppermute x1, waiting for transfers between devices, local(): other = lax.ppermute(sent, 'replica', [(i, i ^ 2) for i in range(replicas)])  4.44 us
    all_to_all x1, waiting for transfers between devices, local(): lax.all_to_all(replica_local_weights[0].reshape(blocks.shape), 'replica',...  3.49 us
    all_to_all x1, waiting for transfers between devices, local(): lax.all_to_all(squares, ('replica', 'fsdp'), 0, 0, axis_index_groups=near...  3.47 us
    ppermute x1, starting transfers between devices, local(): lax.ppermute(mine, 'replica', [(i, i ^ 1) for i in range(replicas)])  3.43 us
  transfers between devices with their start and end apart: 5, of which 3 were waited for; matrix products, arithmetic and copies ran while one was open for 6% of the time, Pallas kernels for 0%

profile of v4, /device:TPU:8, one launch (start us, length us, event | category | flops | bytes accessed | tf_op | source)
XLA Modules:
  0.0 70.3 jit_solution(6472749142394501860)
XLA Ops:
  0.6 0.0 copy-start.1
  0.6 9.2 %all-to-all-start = ((f32[8,128,128]{2,1,0:T(8,128)}), f32[8,128,128]{2,1,0:T(8,128)S(1)}, u32[]{:S(2)}, u32[]{:S(2)}) async-start(f32[8,128,128]{2,1,0:T(8,128)} %bitcast.32), calls=%async_computation | async-start | bytes 1048576 | tf_op jit(solution)/shard_map/all_to_all | solution.py:64
  10.5 0.7 convert_element_type.3
  11.2 0.1 reshape.45
  11.3 0.1 mul.70
  11.4 0.8 %dynamic-slice_bitcast_fusion = f32[128,128]{1,0:T(8,128)S(1)} fusion(f32[8,128,128]{2,1,0:T(8,128)} %bitcast.30, s32[]{:T(128)S(6)} %select_n.34), kind=kLoop, calls=%fused_computation.12 | loop fusion | bytes 131076 | tf_op jit(solution)/shard_map/sub | solution.py:68
  12.2 1.0 %broadcast_multiply_fusion.1 = (f32[1,8192]{1,0:T(1,128)S(1)}, f32[1,8192]{1,0:T(1,128)S(1)}) fusion(f32[64,8192]{1,0:T(8,128)} %param.7, s32[]{:T(128)S(6)} %select_n.35), kind=kLoop, calls=%fused_computation.16 | loop fusion | flops 8192 | bytes 98308 | tf_op jit(solution)/shard_map/mul | solution.py:89
  13.2 3.5 %all-to-all-done = f32[8,128,128]{2,1,0:T(8,128)S(1)} async-done(((f32[8,128,128]{2,1,0:T(8,128)}), f32[8,128,128]{2,1,0:T(8,128)S(1)}, u32[]{:S(2)}, u32[]{:S(2)}) %all-to-all-start) | async-done | bytes 524320 | tf_op jit(solution)/shard_map/all_to_all | solution.py:64
  16.7 0.1 multiply_reduce_fusion
  16.9 3.4 %collective-permute-start = (f32[192,128]{1,0:T(8,128)S(1)}, f32[192,128]{1,0:T(8,128)S(1)}, u32[]{:S(2)}, u32[]{:S(2)}) collective-permute-start(f32[192,128]{1,0:T(8,128)S(1)} %pad_maximum_fusion.1), channel_id=1, source_target_pairs={{0,64},{32,96},{64,0},{96,32},{128,192},{160,224},{192,128},{224,1... | collective-permute-start | bytes 294920 | tf_op jit(solution)/shard_map/ppermute | solution.py:70
  20.3 0.0 copy-done.1
  20.3 0.6 convert_reduce_fusion
  20.9 4.4 %collective-permute-done = f32[192,128]{1,0:T(8,128)S(1)} collective-permute-done((f32[192,128]{1,0:T(8,128)S(1)}, f32[192,128]{1,0:T(8,128)S(1)}, u32[]{:S(2)}, u32[]{:S(2)}) %collective-permute-start) | collective-permute-done | bytes 98336 | tf_op jit(solution)/shard_map/ppermute | solution.py:70
  25.3 1.3 %multiply_reduce_fusion.1 = (f32[]{:T(128)}, f32[128,128]{1,0:T(8,128)S(1)}) fusion(f32[]{:T(128)} %convert_reduce_fusion, f32[128,128]{1,0:T(8,128)S(1)} %multiply_reduce_fusion, f32[192,128]{1,0:T(8,128)S(1)} %collective-permute-done), kind=kLoop, calls=%fused_computation.11 | loop fusion | flops 65535 | bytes 196616 | tf_op jit(solution)/shard_map/reduce_sum | solution.py:75
  26.6 1.3 %broadcast_in_dim.4 = f32[64,1,128]{2,1,0:T(1,128)} broadcast(f32[]{:T(128)} %get-tuple-element.8), dimensions={} | broadcast | bytes 32772 | tf_op jit(solution)/shard_map/broadcast_in_dim | solution.py:75
  27.9 6.0 %all-to-all-start.1 = ((f32[64,1,128]{2,1,0:T(1,128)}), f32[64,1,128]{2,1,0:T(1,128)S(1)}, u32[]{:S(2)}, u32[]{:S(2)}) async-start(f32[64,1,128]{2,1,0:T(1,128)} %broadcast_in_dim.4), calls=%async_computation.1 | async-start | bytes 65536 | tf_op jit(solution)/shard_map/all_to_all | solution.py:78
  34.0 3.4 %collective-permute-start.1 = (f32[256,128]{1,0:T(8,128)S(1)}, f32[256,128]{1,0:T(8,128)S(1)}, u32[]{:S(2)}, u32[]{:S(2)}) collective-permute-start(f32[256,128]{1,0:T(8,128)S(1)} %get-tuple-element.14), channel_id=1, source_target_pairs={{0,32},{32,0},{64,96},{96,64},{128,160},{160,128},{192,224},{224,1... | collective-permute-start | bytes 393224 | tf_op jit(solution)/shard_map/ppermute | solution.py:77
  37.4 3.5 %all-to-all-done.1 = f32[64,1,128]{2,1,0:T(1,128)S(1)} async-done(((f32[64,1,128]{2,1,0:T(1,128)}), f32[64,1,128]{2,1,0:T(1,128)S(1)}, u32[]{:S(2)}, u32[]{:S(2)}) %all-to-all-start.1) | async-done | bytes 32800 | tf_op jit(solution)/shard_map/all_to_all | solution.py:78
  40.9 0.7 slice_reduce_fusion
  41.5 0.0 collective-permute-done.1
  41.6 1.1 %broadcast_in_dim.5 = f32[4,2,256,128]{3,2,1,0:T(8,128)} broadcast(f32[2,256,128]{2,1,0:T(8,128)S(1)} %maximum_select_fusion), dimensions={1,2,3} | broadcast | bytes 1310720 | tf_op jit(solution)/shard_map/broadcast_in_dim | solution.py:82
  42.6 4.9 %all-to-all-start.2 = ((f32[4,2,256,128]{3,2,1,0:T(8,128)}), f32[4,2,256,128]{3,2,1,0:T(8,128)S(1)}, u32[]{:S(2)}, u32[]{:S(2)}) async-start(f32[4,2,256,128]{3,2,1,0:T(8,128)} %broadcast_in_dim.5), calls=%async_computation.2 | async-start | bytes 2097152 | tf_op jit(solution)/shard_map/all_to_all | solution.py:83
  47.5 0.0 copy-start
  47.5 20.4 %psum.7 = f32[]{:T(128)} all-reduce(f32[]{:T(128)} %slice_reduce_fusion), channel_id=1, replica_groups={{0,2,4,6},{1,3,5,7},{8,10,12,14},{9,11,13,15},{16,18,20,22},{17,19,21,2..., use_global_device_ids=true, to_apply=%region_4.5 | all-reduce | flops 1 | bytes 8 | tf_op jit(solution)/shard_map/psum | solution.py:85
  68.6 0.0 all-to-all-done.2
  68.6 0.2 fusion.3
  68.8 0.0 copy-done
  68.8 0.9 %multiply_subtract_fusion = f32[131072]{0:T(1024)} fusion(f32[131072]{0:T(1024)S(1)} %copy-done, f32[131072]{0:T(1024)S(1)} %bitcast.29, f32[131072]{0:T(1024)S(1)} %bitcast.28), kind=kLoop, calls=%fused_computation.1 | loop fusion | flops 655360 | bytes 2097152 | tf_op jit(solution)/shard_map/sub | solution.py:93
  69.7 0.6 bitcast_add_fusion
  (8 shorter events, 0.1 us)
Async XLA Ops:
  0.6 19.7 %copy-start.1 = (s32[16]{0:T(128)S(1)}, s32[16]{0:T(128)}, u32[]{:S(2)}) copy-start(s32[16]{0:T(128)} %param.8) | copy-start | bytes 196
  0.6 16.1 %all-to-all-start = ((f32[8,128,128]{2,1,0:T(8,128)}), f32[8,128,128]{2,1,0:T(8,128)S(1)}, u32[]{:S(2)}, u32[]{:S(2)}) async-start(f32[8,128,128]{2,1,0:T(8,128)} %bitcast.32), calls=%async_computation | async-start | bytes 1048576 | tf_op jit(solution)/shard_map/all_to_all | solution.py:64
  16.9 8.5 %collective-permute-start = (f32[192,128]{1,0:T(8,128)S(1)}, f32[192,128]{1,0:T(8,128)S(1)}, u32[]{:S(2)}, u32[]{:S(2)}) collective-permute-start(f32[192,128]{1,0:T(8,128)S(1)} %pad_maximum_fusion.1), channel_id=1, source_target_pairs={{0,64},{32,96},{64,0},{96,32},{128,192},{160,224},{192,128},{224,1... | collective-permute-start | bytes 294920 | tf_op jit(solution)/shard_map/ppermute | solution.py:70
  27.9 13.0 %all-to-all-start.1 = ((f32[64,1,128]{2,1,0:T(1,128)}), f32[64,1,128]{2,1,0:T(1,128)S(1)}, u32[]{:S(2)}, u32[]{:S(2)}) async-start(f32[64,1,128]{2,1,0:T(1,128)} %broadcast_in_dim.4), calls=%async_computation.1 | async-start | bytes 65536 | tf_op jit(solution)/shard_map/all_to_all | solution.py:78
  34.0 7.6 %collective-permute-start.1 = (f32[256,128]{1,0:T(8,128)S(1)}, f32[256,128]{1,0:T(8,128)S(1)}, u32[]{:S(2)}, u32[]{:S(2)}) collective-permute-start(f32[256,128]{1,0:T(8,128)S(1)} %get-tuple-element.14), channel_id=1, source_target_pairs={{0,32},{32,0},{64,96},{96,64},{128,160},{160,128},{192,224},{224,1... | collective-permute-start | bytes 393224 | tf_op jit(solution)/shard_map/ppermute | solution.py:77
  42.6 26.0 %all-to-all-start.2 = ((f32[4,2,256,128]{3,2,1,0:T(8,128)}), f32[4,2,256,128]{3,2,1,0:T(8,128)S(1)}, u32[]{:S(2)}, u32[]{:S(2)}) async-start(f32[4,2,256,128]{3,2,1,0:T(8,128)} %broadcast_in_dim.5), calls=%async_computation.2 | async-start | bytes 2097152 | tf_op jit(solution)/shard_map/all_to_all | solution.py:83
  47.5 21.3 %copy-start = (f32[131072]{0:T(1024)S(1)}, f32[131072]{0:T(1024)}, u32[]{:S(2)}) copy-start(f32[131072]{0:T(1024)} %param.5) | copy-start | bytes 1572868

commit v5 on v4

--- a/solution.py
+++ b/solution.py
@@ -52,27 +52,29 @@
     frag_total = previous_global_weights.shape[0] * shards
     limit = clip_scale * math.sqrt(frag_total)
     token_weights = reporting_replica_tokens.astype(jnp.float32)
-    reporting_count = jnp.sum(token_weights)
+    token_shares = token_weights / jnp.sum(token_weights)
     blocks = previous_global_weights.reshape(8, -1, lanes)
     depth = blocks.shape[1]
     old_block = lax.dynamic_index_in_dim(blocks, row * 2 + side, 0, keepdims=False)
     state = lax.dynamic_index_in_dim(momentum, target_fragment_index[0], 0, keepdims=False)
     state_piece = state.reshape(-1, lanes)
-    group_weights = lax.dynamic_index_in_dim(
-        token_weights.reshape(4, 2, 2), half, 1, keepdims=False
+    group_shares = lax.dynamic_index_in_dim(
+        token_shares.reshape(4, 2, 2), half, 1, keepdims=False
     ).reshape(8)
     received = lax.all_to_all(
         replica_local_weights[0].reshape(blocks.shape),
         "replica", 0, 0, axis_index_groups=block_groups(), tiled=True,
     )
-    partial = jnp.sum(group_weights[:, None, None] * (old_block[None] - received), 0)
+    partial = jnp.sum(group_shares[:, None, None] * (old_block[None] - received), 0)
     sent = jnp.concatenate([partial, state_piece], 0)
     other = lax.ppermute(sent, "replica", [(i, i ^ 2) for i in range(replicas)])
-    average = (partial + other[:depth]) / reporting_count
+    average = partial + other[:depth]
     pair = jnp.stack([state_piece, other[depth:]])
     pair = jnp.where(half == 0, pair, pair[::-1]).reshape(depth, lanes)
     near = near_groups(shards)
-    squares = jnp.broadcast_to(jnp.sum(average * average), (len(near[0]), 1, lanes))
+    rows = jnp.sum(average * average, 0, keepdims=True)
+    rows = jnp.dot(rows, jnp.ones((lanes, lanes), jnp.float32), precision=lax.Precision.HIGHEST)
+    squares = jnp.broadcast_to(rows[None], (len(near[0]), 1, lanes))
     mine = jnp.concatenate([average, pair], 0)
     beside = lax.ppermute(mine, "replica", [(i, i ^ 1) for i in range(replicas)])
     squares = lax.all_to_all(squares, ("replica", "fsdp"), 0, 0, axis_index_groups=near, tiled=True)

time: 70.8 us -> 69.1 us (0.976)
  waiting for transfers between devices: 11.4 us -> 10.1 us
    all_to_all x1, waiting for transfers between devices: 3.49 us -> 1.58 us  [local(): lax.all_to_all(replica_local_weights[0].reshape(blocks.shape), 'replica',...]
    div x0 -> x1, other arithmetic: none -> 1.3 us  [local(): token_shares = token_weights / jnp.sum(token_weights)]
  transfers between devices with their start and end apart: 5 -> 5, of which waited for: 3 -> 3; matrix products, arithmetic and copies ran while one was open for 6% -> 8% of each run, Pallas kernels for 0% -> 0%
where the time goes in v5:
time: 69.1 us; the launch traced here: 68.6 us
  starting transfers between devices  26.9 us (39%)
  blocking collectives  20.4 us (30%)
  waiting for transfers between devices  10.1 us (15%)
  other arithmetic  6.12 us (9%)
  local copies, waits for them, and re-layouts  2.81 us (4%)
  between operations  2.11 us (3%)
    psum x1, blocking collectives, local(): squares = lax.psum(squares, 'fsdp', axis_index_groups=far_groups())  20.4 us
    all_to_all x1, starting transfers between devices, local(): lax.all_to_all(replica_local_weights[0].reshape(blocks.shape), 'replica',...  9.24 us
    all_to_all x1, starting transfers between devices, local(): lax.all_to_all(squares, ('replica', 'fsdp'), 0, 0, axis_index_groups=near...  6 us
    ppermute x1, waiting for transfers between devices, local(): other = lax.ppermute(sent, 'replica', [(i, i ^ 2) for i in range(replicas)])  5.05 us
    all_to_all x1, starting transfers between devices, local(): lax.all_to_all(sent, 'replica', 0, 0, axis_index_groups=line_groups(), ti...  4.88 us
    all_to_all x1, waiting for transfers between devices, local(): lax.all_to_all(squares, ('replica', 'fsdp'), 0, 0, axis_index_groups=near...  3.47 us
    ppermute x1, starting transfers between devices, local(): lax.ppermute(mine, 'replica', [(i, i ^ 1) for i in range(replicas)])  3.43 us
    ppermute x1, starting transfers between devices, local(): other = lax.ppermute(sent, 'replica', [(i, i ^ 2) for i in range(replicas)])  3.4 us
  transfers between devices with their start and end apart: 5, of which 3 were waited for; matrix products, arithmetic and copies ran while one was open for 8% of the time, Pallas kernels for 0%

profile of v5, /device:TPU:8, one launch (start us, length us, event | category | flops | bytes accessed | tf_op | source)
XLA Modules:
  0.0 68.6 jit_solution(5866752088872920184)
XLA Ops:
  0.6 9.2 %all-to-all-start = ((f32[8,128,128]{2,1,0:T(8,128)}), f32[8,128,128]{2,1,0:T(8,128)S(1)}, u32[]{:S(2)}, u32[]{:S(2)}) async-start(f32[8,128,128]{2,1,0:T(8,128)} %bitcast.37), calls=%async_computation | async-start | bytes 1048576 | tf_op jit(solution)/shard_map/all_to_all | solution.py:64
  10.5 1.3 %convert_reduce_fusion = f32[]{:T(128)} fusion(s32[16]{0:T(128)} %param.8), kind=kLoop, calls=%fused_computation.21 | loop fusion | flops 31 | bytes 68 | tf_op jit(solution)/shard_map/reduce_sum | solution.py:55
  11.8 1.3 %convert_divide_fusion = f32[16]{0:T(128)S(1)} fusion(s32[16]{0:T(128)} %param.8, f32[]{:T(128)} %convert_reduce_fusion), kind=kLoop, calls=%fused_computation.20 | loop fusion | flops 32 | bytes 132 | tf_op jit(solution)/shard_map/div | solution.py:55
  13.1 0.1 reshape.52
  13.2 0.1 mul.70
  13.3 0.9 %dynamic-slice_bitcast_fusion = f32[128,128]{1,0:T(8,128)S(1)} fusion(f32[8,128,128]{2,1,0:T(8,128)} %bitcast.35, s32[]{:T(128)S(6)} %select_n.34), kind=kLoop, calls=%fused_computation.12 | loop fusion | bytes 131076 | tf_op jit(solution)/shard_map/sub | solution.py:68
  14.1 1.0 %broadcast_multiply_fusion.1 = (f32[1,8192]{1,0:T(1,128)S(1)}, f32[1,8192]{1,0:T(1,128)S(1)}) fusion(f32[64,8192]{1,0:T(8,128)} %param.7, s32[]{:T(128)S(6)} %select_n.35), kind=kLoop, calls=%fused_computation.17 | loop fusion | flops 8192 | bytes 98308 | tf_op jit(solution)/shard_map/mul | solution.py:91
  15.1 1.6 %all-to-all-done = f32[8,128,128]{2,1,0:T(8,128)S(1)} async-done(((f32[8,128,128]{2,1,0:T(8,128)}), f32[8,128,128]{2,1,0:T(8,128)S(1)}, u32[]{:S(2)}, u32[]{:S(2)}) %all-to-all-start) | async-done | bytes 524320 | tf_op jit(solution)/shard_map/all_to_all | solution.py:64
  16.7 0.1 multiply_reduce_fusion
  16.9 3.4 %collective-permute-start = (f32[192,128]{1,0:T(8,128)S(1)}, f32[192,128]{1,0:T(8,128)S(1)}, u32[]{:S(2)}, u32[]{:S(2)}) collective-permute-start(f32[192,128]{1,0:T(8,128)S(1)} %pad_maximum_fusion.1), channel_id=1, source_target_pairs={{0,64},{32,96},{64,0},{96,32},{128,192},{160,224},{192,128},{224,1... | collective-permute-start | bytes 294920 | tf_op jit(solution)/shard_map/ppermute | solution.py:70
  20.3 5.0 %collective-permute-done = f32[192,128]{1,0:T(8,128)S(1)} collective-permute-done((f32[192,128]{1,0:T(8,128)S(1)}, f32[192,128]{1,0:T(8,128)S(1)}, u32[]{:S(2)}, u32[]{:S(2)}) %collective-permute-start) | collective-permute-done | bytes 98336 | tf_op jit(solution)/shard_map/ppermute | solution.py:70
  25.4 0.1 convolution_bitcast_fusion
  25.5 0.7 broadcast_in_dim.7
  26.1 6.0 %all-to-all-start.1 = ((f32[64,1,128]{2,1,0:T(1,128)}), f32[64,1,128]{2,1,0:T(1,128)S(1)}, u32[]{:S(2)}, u32[]{:S(2)}) async-start(f32[64,1,128]{2,1,0:T(1,128)} %broadcast_in_dim.7), calls=%async_computation.1 | async-start | bytes 65536 | tf_op jit(solution)/shard_map/all_to_all | solution.py:80
  32.2 3.4 %collective-permute-start.1 = (f32[256,128]{1,0:T(8,128)S(1)}, f32[256,128]{1,0:T(8,128)S(1)}, u32[]{:S(2)}, u32[]{:S(2)}) collective-permute-start(f32[256,128]{1,0:T(8,128)S(1)} %get-tuple-element.14), channel_id=1, source_target_pairs={{0,32},{32,0},{64,96},{96,64},{128,160},{160,128},{192,224},{224,1... | collective-permute-start | bytes 393224 | tf_op jit(solution)/shard_map/ppermute | solution.py:79
  35.7 3.5 %all-to-all-done.1 = f32[64,1,128]{2,1,0:T(1,128)S(1)} async-done(((f32[64,1,128]{2,1,0:T(1,128)}), f32[64,1,128]{2,1,0:T(1,128)S(1)}, u32[]{:S(2)}, u32[]{:S(2)}) %all-to-all-start.1) | async-done | bytes 32800 | tf_op jit(solution)/shard_map/all_to_all | solution.py:80
  39.1 0.7 slice_reduce_fusion
  39.8 0.0 collective-permute-done.1
  39.8 1.1 %broadcast_in_dim.8 = f32[4,2,256,128]{3,2,1,0:T(8,128)} broadcast(f32[2,256,128]{2,1,0:T(8,128)S(1)} %maximum_select_fusion), dimensions={1,2,3} | broadcast | bytes 1310720 | tf_op jit(solution)/shard_map/broadcast_in_dim | solution.py:84
  40.9 4.9 %all-to-all-start.2 = ((f32[4,2,256,128]{3,2,1,0:T(8,128)}), f32[4,2,256,128]{3,2,1,0:T(8,128)S(1)}, u32[]{:S(2)}, u32[]{:S(2)}) async-start(f32[4,2,256,128]{3,2,1,0:T(8,128)} %broadcast_in_dim.8), calls=%async_computation.2 | async-start | bytes 2097152 | tf_op jit(solution)/shard_map/all_to_all | solution.py:85
  45.8 0.0 copy-start
  45.8 20.4 %psum.7 = f32[]{:T(128)} all-reduce(f32[]{:T(128)} %slice_reduce_fusion), channel_id=1, replica_groups={{0,2,4,6},{1,3,5,7},{8,10,12,14},{9,11,13,15},{16,18,20,22},{17,19,21,2..., use_global_device_ids=true, to_apply=%region_4.5 | all-reduce | flops 1 | bytes 8 | tf_op jit(solution)/shard_map/psum | solution.py:87
  66.8 0.0 all-to-all-done.2
  66.9 0.2 fusion.4
  67.1 0.0 copy-done
  67.1 0.9 %multiply_subtract_fusion = f32[131072]{0:T(1024)} fusion(f32[131072]{0:T(1024)S(1)} %copy-done, f32[131072]{0:T(1024)S(1)} %bitcast.34, f32[131072]{0:T(1024)S(1)} %bitcast.33), kind=kLoop, calls=%fused_computation.2 | loop fusion | flops 655360 | bytes 2097152 | tf_op jit(solution)/shard_map/sub | solution.py:95
  68.0 0.6 bitcast_add_fusion
  (9 shorter events, 0.2 us)
Async XLA Ops:
  0.6 16.1 %all-to-all-start = ((f32[8,128,128]{2,1,0:T(8,128)}), f32[8,128,128]{2,1,0:T(8,128)S(1)}, u32[]{:S(2)}, u32[]{:S(2)}) async-start(f32[8,128,128]{2,1,0:T(8,128)} %bitcast.37), calls=%async_computation | async-start | bytes 1048576 | tf_op jit(solution)/shard_map/all_to_all | solution.py:64
  16.9 8.5 %collective-permute-start = (f32[192,128]{1,0:T(8,128)S(1)}, f32[192,128]{1,0:T(8,128)S(1)}, u32[]{:S(2)}, u32[]{:S(2)}) collective-permute-start(f32[192,128]{1,0:T(8,128)S(1)} %pad_maximum_fusion.1), channel_id=1, source_target_pairs={{0,64},{32,96},{64,0},{96,32},{128,192},{160,224},{192,128},{224,1... | collective-permute-start | bytes 294920 | tf_op jit(solution)/shard_map/ppermute | solution.py:70
  26.1 13.0 %all-to-all-start.1 = ((f32[64,1,128]{2,1,0:T(1,128)}), f32[64,1,128]{2,1,0:T(1,128)S(1)}, u32[]{:S(2)}, u32[]{:S(2)}) async-start(f32[64,1,128]{2,1,0:T(1,128)} %broadcast_in_dim.7), calls=%async_computation.1 | async-start | bytes 65536 | tf_op jit(solution)/shard_map/all_to_all | solution.py:80
  32.2 7.6 %collective-permute-start.1 = (f32[256,128]{1,0:T(8,128)S(1)}, f32[256,128]{1,0:T(8,128)S(1)}, u32[]{:S(2)}, u32[]{:S(2)}) collective-permute-start(f32[256,128]{1,0:T(8,128)S(1)} %get-tuple-element.14), channel_id=1, source_target_pairs={{0,32},{32,0},{64,96},{96,64},{128,160},{160,128},{192,224},{224,1... | collective-permute-start | bytes 393224 | tf_op jit(solution)/shard_map/ppermute | solution.py:79
  40.9 26.0 %all-to-all-start.2 = ((f32[4,2,256,128]{3,2,1,0:T(8,128)}), f32[4,2,256,128]{3,2,1,0:T(8,128)S(1)}, u32[]{:S(2)}, u32[]{:S(2)}) async-start(f32[4,2,256,128]{3,2,1,0:T(8,128)} %broadcast_in_dim.8), calls=%async_computation.2 | async-start | bytes 2097152 | tf_op jit(solution)/shard_map/all_to_all | solution.py:85
  45.8 21.3 %copy-start = (f32[131072]{0:T(1024)S(1)}, f32[131072]{0:T(1024)}, u32[]{:S(2)}) copy-start(f32[131072]{0:T(1024)} %param.5) | copy-start | bytes 1572868

commit v6 on v5

--- a/solution.py
+++ b/solution.py
@@ -38,6 +38,12 @@
     return [[x * 8 + far * 2 + core for far in range(4)] for x in range(4) for core in range(2)]
 
 
+def lane_total(row):
+    ones = jnp.ones((lanes, lanes), jnp.float32)
+    total = jnp.dot(row * 2.0**-40, ones, precision=lax.Precision.HIGHEST) * 2.0**40
+    return jnp.where(jnp.isnan(total), jnp.inf, total)
+
+
 def local(
     previous_global_weights,
     replica_local_weights,
@@ -52,7 +58,9 @@
     frag_total = previous_global_weights.shape[0] * shards
     limit = clip_scale * math.sqrt(frag_total)
     token_weights = reporting_replica_tokens.astype(jnp.float32)
-    token_shares = token_weights / jnp.sum(token_weights)
+    ones = jnp.ones((replicas, replicas), jnp.float32)
+    counts = jnp.dot(token_weights[None], ones, precision=lax.Precision.HIGHEST)
+    token_shares = token_weights / counts[0]
     blocks = previous_global_weights.reshape(8, -1, lanes)
     depth = blocks.shape[1]
     old_block = lax.dynamic_index_in_dim(blocks, row * 2 + side, 0, keepdims=False)
@@ -61,24 +69,22 @@
     group_shares = lax.dynamic_index_in_dim(
         token_shares.reshape(4, 2, 2), half, 1, keepdims=False
     ).reshape(8)
+    other_state = lax.ppermute(state_piece, "replica", [(i, i ^ 2) for i in range(replicas)])
     received = lax.all_to_all(
         replica_local_weights[0].reshape(blocks.shape),
         "replica", 0, 0, axis_index_groups=block_groups(), tiled=True,
     )
     partial = jnp.sum(group_shares[:, None, None] * (old_block[None] - received), 0)
-    sent = jnp.concatenate([partial, state_piece], 0)
-    other = lax.ppermute(sent, "replica", [(i, i ^ 2) for i in range(replicas)])
-    average = partial + other[:depth]
-    pair = jnp.stack([state_piece, other[depth:]])
+    average = partial + lax.ppermute(partial, "replica", [(i, i ^ 2) for i in range(replicas)])
+    pair = jnp.stack([state_piece, other_state])
     pair = jnp.where(half == 0, pair, pair[::-1]).reshape(depth, lanes)
     near = near_groups(shards)
-    rows = jnp.sum(average * average, 0, keepdims=True)
-    rows = jnp.dot(rows, jnp.ones((lanes, lanes), jnp.float32), precision=lax.Precision.HIGHEST)
-    squares = jnp.broadcast_to(rows[None], (len(near[0]), 1, lanes))
+    squares = lane_total(jnp.sum(average * average, 0, keepdims=True))
+    squares = jnp.broadcast_to(squares[None], (len(near[0]), 1, lanes))
     mine = jnp.concatenate([average, pair], 0)
     beside = lax.ppermute(mine, "replica", [(i, i ^ 1) for i in range(replicas)])
     squares = lax.all_to_all(squares, ("replica", "fsdp"), 0, 0, axis_index_groups=near, tiled=True)
-    squares = jnp.sum(squares[:, 0, 0])
+    squares = jnp.sum(squares[:32, 0] + squares[32:, 0], 0, keepdims=True)
     sent = jnp.where(side == 0, jnp.stack([mine, beside]), jnp.stack([beside, mine]))
     sent, squares = lax.optimization_barrier((sent, squares))
     sent = jnp.broadcast_to(sent[None], (4,) + sent.shape)

time: 69.1 us -> 67.4 us (0.975)
  other arithmetic: 6.12 us -> 2.86 us
  starting transfers between devices: 26.9 us -> 29.7 us
  blocking collectives: 20.4 us -> 19.2 us
  matrix products: 0.13 us -> 0.99 us
    ppermute x1 -> x2, starting transfers between devices: 3.4 us -> 5.45 us  [the longest x1 3.22 us: local(): lax.ppermute(partial, 'replica', [(i, i ^ 2) for i in range(replicas)])]
    reduce_sum x3 -> x2, other arithmetic: 1.97 us -> 0.06 us  [the longest x1 0.03 us: local(): squares = lane_total(jnp.sum(average * average, 0, keepdims=True))]
    div x1 -> x0, other arithmetic: 1.3 us -> none  [local(): token_shares = token_weights / jnp.sum(token_weights)]
    psum x1, blocking collectives: 20.4 us -> 19.2 us  [local(): squares = lax.psum(squares, 'fsdp', axis_index_groups=far_groups())]
    dot_general x1 -> x2, matrix products: 0.13 us -> 0.99 us  [the longest x1 0.86 us: local(): counts = jnp.dot(token_weights[None], ones, precision=lax.Precision.HIGHEST)]
    all_to_all x1, starting transfers between devices: 6 us -> 6.73 us  [local(): lax.all_to_all(squares, ('replica', 'fsdp'), 0, 0, axis_index_groups=near...]
    ppermute x1 -> x2, waiting for transfers between devices: 5.05 us -> 4.51 us  [the longest x1 4.51 us: local(): lax.ppermute(partial, 'replica', [(i, i ^ 2) for i in range(replicas)])]
  transfers between devices with their start and end apart: 5 -> 6, of which waited for: 3 -> 4; matrix products, arithmetic and copies ran while one was open for 8% -> 5% of each run, Pallas kernels for 0% -> 0%
where the time goes in v6:
time: 67.4 us; the launch traced here: 66.9 us
  starting transfers between devices  29.7 us (44%)
  blocking collectives  19.2 us (28%)
  waiting for transfers between devices  9.79 us (15%)
  other arithmetic  2.86 us (4%)
  local copies, waits for them, and re-layouts  2.85 us (4%)
  between operations  1.42 us (2%)
  matrix products  0.99 us (1%)
    psum x1, blocking collectives, local(): squares = lax.psum(squares, 'fsdp', axis_index_groups=far_groups())  19.2 us
    all_to_all x1, starting transfers between devices, local(): lax.all_to_all(replica_local_weights[0].reshape(blocks.shape), 'replica',...  9.24 us
    all_to_all x1, starting transfers between devices, local(): lax.all_to_all(squares, ('replica', 'fsdp'), 0, 0, axis_index_groups=near...  6.73 us
    all_to_all x1, starting transfers between devices, local(): lax.all_to_all(sent, 'replica', 0, 0, axis_index_groups=line_groups(), ti...  4.89 us
    ppermute x1, waiting for transfers between devices, local(): lax.ppermute(partial, 'replica', [(i, i ^ 2) for i in range(replicas)])  4.51 us
    all_to_all x1, waiting for transfers between devices, local(): lax.all_to_all(squares, ('replica', 'fsdp'), 0, 0, axis_index_groups=near...  3.5 us
    ppermute x1, starting transfers between devices, local(): lax.ppermute(mine, 'replica', [(i, i ^ 1) for i in range(replicas)])  3.41 us
    ppermute x1, starting transfers between devices, local(): lax.ppermute(partial, 'replica', [(i, i ^ 2) for i in range(replicas)])  3.22 us
  transfers between devices with their start and end apart: 6, of which 4 were waited for; matrix products, arithmetic and copies ran while one was open for 5% of the time, Pallas kernels for 0%

profile of v6, /device:TPU:8, one launch (start us, length us, event | category | flops | bytes accessed | tf_op | source)
XLA Modules:
  0.0 66.9 jit_solution(8992746263660555823)
XLA Ops:
  0.6 9.2 %all-to-all-start = ((f32[8,128,128]{2,1,0:T(8,128)}), f32[8,128,128]{2,1,0:T(8,128)S(1)}, u32[]{:S(2)}, u32[]{:S(2)}) async-start(f32[8,128,128]{2,1,0:T(8,128)} %bitcast.57), calls=%async_computation | async-start | bytes 1048576 | tf_op jit(solution)/shard_map/all_to_all | solution.py:73
  10.5 1.0 %broadcast_multiply_fusion = (f32[1,8192]{1,0:T(1,128)S(1)}, f32[1,8192]{1,0:T(1,128)S(1)}) fusion(f32[64,8192]{1,0:T(8,128)} %param.7, s32[]{:T(128)S(6)} %select_n.41), kind=kLoop, calls=%fused_computation.17 | loop fusion | flops 8192 | bytes 98308 | tf_op jit(solution)/shard_map/mul | solution.py:97
  11.5 2.2 %collective-permute-start.1 = (f32[64,128]{1,0:T(8,128)S(1)}, f32[64,128]{1,0:T(8,128)S(1)}, u32[]{:S(2)}, u32[]{:S(2)}) collective-permute-start(f32[64,128]{1,0:T(8,128)S(1)} %bitcast.61), channel_id=1, source_target_pairs={{0,64},{32,96},{64,0},{96,32},{128,192},{160,224},{192,128},{224,1... | collective-permute-start | bytes 98312 | tf_op jit(solution)/shard_map/ppermute | solution.py:72
  13.8 0.9 %fusion.1 = f32[16]{0:T(128)S(1)} fusion(s32[16]{0:T(128)} %param.8), kind=kOutput, calls=%fused_computation.3 | convolution fusion | flops 3120 | bytes 128 | tf_op jit(solution)/shard_map/dot_general | solution.py:62
  14.6 0.1 reshape.62
  14.8 0.1 mul.90
  14.8 0.9 %dynamic-slice_bitcast_fusion = f32[128,128]{1,0:T(8,128)S(1)} fusion(f32[8,128,128]{2,1,0:T(8,128)} %bitcast.56, s32[]{:T(128)S(6)} %select_n.39), kind=kLoop, calls=%fused_computation.12 | loop fusion | bytes 131076 | tf_op jit(solution)/shard_map/sub | solution.py:77
  15.7 1.3 %all-to-all-done = f32[8,128,128]{2,1,0:T(8,128)S(1)} async-done(((f32[8,128,128]{2,1,0:T(8,128)}), f32[8,128,128]{2,1,0:T(8,128)S(1)}, u32[]{:S(2)}, u32[]{:S(2)}) %all-to-all-start) | async-done | bytes 524320 | tf_op jit(solution)/shard_map/all_to_all | solution.py:73
  17.0 0.1 multiply_reduce_fusion
  17.1 3.2 %collective-permute-start = (f32[128,128]{1,0:T(8,128)S(1)}, f32[128,128]{1,0:T(8,128)S(1)}, u32[]{:S(2)}, u32[]{:S(2)}) collective-permute-start(f32[128,128]{1,0:T(8,128)S(1)} %multiply_reduce_fusion), channel_id=1, source_target_pairs={{0,64},{32,96},{64,0},{96,32},{128,192},{160,224},{192,128},{224,1... | collective-permute-start | bytes 196616 | tf_op jit(solution)/shard_map/ppermute | solution.py:78
  20.3 0.0 collective-permute-done.1
  20.4 4.5 %collective-permute-done = f32[128,128]{1,0:T(8,128)S(1)} collective-permute-done((f32[128,128]{1,0:T(8,128)S(1)}, f32[128,128]{1,0:T(8,128)S(1)}, u32[]{:S(2)}, u32[]{:S(2)}) %collective-permute-start) | collective-permute-done | bytes 65568 | tf_op jit(solution)/shard_map/ppermute | solution.py:78
  24.9 0.1 compare_select_fusion
  25.0 0.7 broadcast_in_dim.32
  25.7 6.7 %all-to-all-start.1 = ((f32[64,1,128]{2,1,0:T(1,128)}), f32[64,1,128]{2,1,0:T(1,128)S(1)}, u32[]{:S(2)}, u32[]{:S(2)}) async-start(f32[64,1,128]{2,1,0:T(1,128)} %broadcast_in_dim.32), calls=%async_computation.1 | async-start | bytes 65536 | tf_op jit(solution)/shard_map/all_to_all | solution.py:86
  32.5 3.4 %collective-permute-start.2 = (f32[256,128]{1,0:T(8,128)S(1)}, f32[256,128]{1,0:T(8,128)S(1)}, u32[]{:S(2)}, u32[]{:S(2)}) collective-permute-start(f32[256,128]{1,0:T(8,128)S(1)} %get-tuple-element.13), channel_id=1, source_target_pairs={{0,32},{32,0},{64,96},{96,64},{128,160},{160,128},{192,224},{224,1... | collective-permute-start | bytes 393224 | tf_op jit(solution)/shard_map/ppermute | solution.py:85
  35.9 3.5 %all-to-all-done.1 = f32[64,1,128]{2,1,0:T(1,128)S(1)} async-done(((f32[64,1,128]{2,1,0:T(1,128)}), f32[64,1,128]{2,1,0:T(1,128)S(1)}, u32[]{:S(2)}, u32[]{:S(2)}) %all-to-all-start.1) | async-done | bytes 32800 | tf_op jit(solution)/shard_map/all_to_all | solution.py:86
  39.4 0.5 collective-permute-done.2
  40.0 1.1 %broadcast_in_dim.34 = f32[4,2,256,128]{3,2,1,0:T(8,128)} broadcast(f32[2,256,128]{2,1,0:T(8,128)S(1)} %maximum_select_fusion), dimensions={1,2,3} | broadcast | bytes 1310720 | tf_op jit(solution)/shard_map/broadcast_in_dim | solution.py:90
  41.0 4.9 %all-to-all-start.2 = ((f32[4,2,256,128]{3,2,1,0:T(8,128)}), f32[4,2,256,128]{3,2,1,0:T(8,128)S(1)}, u32[]{:S(2)}, u32[]{:S(2)}) async-start(f32[4,2,256,128]{3,2,1,0:T(8,128)} %broadcast_in_dim.34), calls=%async_computation.2 | async-start | bytes 2097152 | tf_op jit(solution)/shard_map/all_to_all | solution.py:91
  45.9 0.0 copy-start
  45.9 19.2 %psum.7 = f32[1,128]{1,0:T(1,128)S(1)} all-reduce(f32[1,128]{1,0:T(1,128)S(1)} %bitcast.65), channel_id=1, replica_groups={{0,2,4,6},{1,3,5,7},{8,10,12,14},{9,11,13,15},{16,18,20,22},{17,19,21,2..., use_global_device_ids=true, to_apply=%region_3.4 | all-reduce | flops 128 | bytes 1024 | tf_op jit(solution)/shard_map/psum | solution.py:93
  65.2 0.0 all-to-all-done.2
  65.2 0.1 fusion.12
  65.4 0.0 copy-done
  65.4 0.9 %multiply_subtract_fusion = f32[131072]{0:T(1024)} fusion(f32[131072]{0:T(1024)S(1)} %copy-done, f32[131072]{0:T(1024)S(1)} %bitcast.53, f32[131072]{0:T(1024)S(1)} %bitcast.51, f32[131072]{0:T(1024)S(1)} %bitcast.54), kind=kLoop, calls=%fused_computation.5 | loop fusion | flops 786432 | bytes 2621440 | tf_op jit(solution)/shard_map/sub | solution.py:101
  66.3 0.6 fusion.2
  (11 shorter events, 0.3 us)
Async XLA Ops:
  0.6 16.4 %all-to-all-start = ((f32[8,128,128]{2,1,0:T(8,128)}), f32[8,128,128]{2,1,0:T(8,128)S(1)}, u32[]{:S(2)}, u32[]{:S(2)}) async-start(f32[8,128,128]{2,1,0:T(8,128)} %bitcast.57), calls=%async_computation | async-start | bytes 1048576 | tf_op jit(solution)/shard_map/all_to_all | solution.py:73
  11.5 8.8 %collective-permute-start.1 = (f32[64,128]{1,0:T(8,128)S(1)}, f32[64,128]{1,0:T(8,128)S(1)}, u32[]{:S(2)}, u32[]{:S(2)}) collective-permute-start(f32[64,128]{1,0:T(8,128)S(1)} %bitcast.61), channel_id=1, source_target_pairs={{0,64},{32,96},{64,0},{96,32},{128,192},{160,224},{192,128},{224,1... | collective-permute-start | bytes 98312 | tf_op jit(solution)/shard_map/ppermute | solution.py:72
  17.1 7.8 %collective-permute-start = (f32[128,128]{1,0:T(8,128)S(1)}, f32[128,128]{1,0:T(8,128)S(1)}, u32[]{:S(2)}, u32[]{:S(2)}) collective-permute-start(f32[128,128]{1,0:T(8,128)S(1)} %multiply_reduce_fusion), channel_id=1, source_target_pairs={{0,64},{32,96},{64,0},{96,32},{128,192},{160,224},{192,128},{224,1... | collective-permute-start | bytes 196616 | tf_op jit(solution)/shard_map/ppermute | solution.py:78
  25.7 13.7 %all-to-all-start.1 = ((f32[64,1,128]{2,1,0:T(1,128)}), f32[64,1,128]{2,1,0:T(1,128)S(1)}, u32[]{:S(2)}, u32[]{:S(2)}) async-start(f32[64,1,128]{2,1,0:T(1,128)} %broadcast_in_dim.32), calls=%async_computation.1 | async-start | bytes 65536 | tf_op jit(solution)/shard_map/all_to_all | solution.py:86
  32.5 7.4 %collective-permute-start.2 = (f32[256,128]{1,0:T(8,128)S(1)}, f32[256,128]{1,0:T(8,128)S(1)}, u32[]{:S(2)}, u32[]{:S(2)}) collective-permute-start(f32[256,128]{1,0:T(8,128)S(1)} %get-tuple-element.13), channel_id=1, source_target_pairs={{0,32},{32,0},{64,96},{96,64},{128,160},{160,128},{192,224},{224,1... | collective-permute-start | bytes 393224 | tf_op jit(solution)/shard_map/ppermute | solution.py:85
  41.0 24.2 %all-to-all-start.2 = ((f32[4,2,256,128]{3,2,1,0:T(8,128)}), f32[4,2,256,128]{3,2,1,0:T(8,128)S(1)}, u32[]{:S(2)}, u32[]{:S(2)}) async-start(f32[4,2,256,128]{3,2,1,0:T(8,128)} %broadcast_in_dim.34), calls=%async_computation.2 | async-start | bytes 2097152 | tf_op jit(solution)/shard_map/all_to_all | solution.py:91
  45.9 19.5 %copy-start = (f32[131072]{0:T(1024)S(1)}, f32[131072]{0:T(1024)}, u32[]{:S(2)}) copy-start(f32[131072]{0:T(1024)} %param.5) | copy-start | bytes 1572868

commit v7 on v6

--- a/solution.py
+++ b/solution.py
@@ -76,16 +76,21 @@
     )
     partial = jnp.sum(group_shares[:, None, None] * (old_block[None] - received), 0)
     average = partial + lax.ppermute(partial, "replica", [(i, i ^ 2) for i in range(replicas)])
+    other_state, _ = lax.optimization_barrier((other_state, partial))
     pair = jnp.stack([state_piece, other_state])
     pair = jnp.where(half == 0, pair, pair[::-1]).reshape(depth, lanes)
+    beside_pair = lax.ppermute(pair, "replica", [(i, i ^ 1) for i in range(replicas)])
     near = near_groups(shards)
     squares = lane_total(jnp.sum(average * average, 0, keepdims=True))
     squares = jnp.broadcast_to(squares[None], (len(near[0]), 1, lanes))
-    mine = jnp.concatenate([average, pair], 0)
-    beside = lax.ppermute(mine, "replica", [(i, i ^ 1) for i in range(replicas)])
+    beside = lax.ppermute(average, "replica", [(i, i ^ 1) for i in range(replicas)])
     squares = lax.all_to_all(squares, ("replica", "fsdp"), 0, 0, axis_index_groups=near, tiled=True)
     squares = jnp.sum(squares[:32, 0] + squares[32:, 0], 0, keepdims=True)
-    sent = jnp.where(side == 0, jnp.stack([mine, beside]), jnp.stack([beside, mine]))
+    beside, squares = lax.optimization_barrier((beside, squares))
+    first = side == 0
+    averages = jnp.where(first, jnp.stack([average, beside]), jnp.stack([beside, average]))
+    pairs = jnp.where(first, jnp.stack([pair, beside_pair]), jnp.stack([beside_pair, pair]))
+    sent = jnp.concatenate([averages, pairs], 1)
     sent, squares = lax.optimization_barrier((sent, squares))
     sent = jnp.broadcast_to(sent[None], (4,) + sent.shape)
     parts = lax.all_to_all(sent, "replica", 0, 0, axis_index_groups=line_groups(), tiled=True)

time: 67.4 us -> 67 us (level)
  waiting for transfers between devices: 9.79 us -> 5.92 us
  starting transfers between devices: 29.7 us -> 33.5 us
    ppermute x1, waiting for transfers between devices: 4.51 us -> 1.11 us  [local(): lax.ppermute(partial, 'replica', [(i, i ^ 2) for i in range(replicas)])]
    ppermute x1 -> x2, starting transfers between devices: 3.41 us -> 6.79 us  [the longest x1 3.41 us: local(): lax.ppermute(average, 'replica', [(i, i ^ 1) for i in range(replicas)])]
  transfers between devices with their start and end apart: 6 -> 7, of which waited for: 4 -> 3; matrix products, arithmetic and copies ran while one was open for 5% -> 6% of each run, Pallas kernels for 0% -> 0%
where the time goes in v7:
time: 67 us; the launch traced here: 66.5 us
  starting transfers between devices  33.5 us (50%)
  blocking collectives  18.9 us (28%)
  waiting for transfers between devices  5.92 us (9%)
  other arithmetic  2.87 us (4%)
  local copies, waits for them, and re-layouts  2.85 us (4%)
  between operations  1.46 us (2%)
  matrix products  0.99 us (1%)
    psum x1, blocking collectives, local(): squares = lax.psum(squares, 'fsdp', axis_index_groups=far_groups())  18.9 us
    all_to_all x1, starting transfers between devices, local(): lax.all_to_all(replica_local_weights[0].reshape(blocks.shape), 'replica',...  9.24 us
    all_to_all x1, starting transfers between devices, local(): lax.all_to_all(squares, ('replica', 'fsdp'), 0, 0, axis_index_groups=near...  7.16 us
    all_to_all x1, starting transfers between devices, local(): lax.all_to_all(sent, 'replica', 0, 0, axis_index_groups=line_groups(), ti...  4.88 us
    all_to_all x1, waiting for transfers between devices, local(): lax.all_to_all(squares, ('replica', 'fsdp'), 0, 0, axis_index_groups=near...  3.51 us
    ppermute x1, starting transfers between devices, local(): lax.ppermute(average, 'replica', [(i, i ^ 1) for i in range(replicas)])  3.41 us
    ppermute x1, starting transfers between devices, local(): lax.ppermute(pair, 'replica', [(i, i ^ 1) for i in range(replicas)])  3.38 us
    ppermute x1, starting transfers between devices, local(): lax.ppermute(partial, 'replica', [(i, i ^ 2) for i in range(replicas)])  3.22 us
  transfers between devices with their start and end apart: 7, of which 3 were waited for; matrix products, arithmetic and copies ran while one was open for 6% of the time, Pallas kernels for 0%

profile of v7, /device:TPU:8, one launch (start us, length us, event | category | flops | bytes accessed | tf_op | source)
XLA Modules:
  0.0 66.5 jit_solution(10491922198060071074)
XLA Ops:
  0.6 9.2 %all-to-all-start = ((f32[8,128,128]{2,1,0:T(8,128)}), f32[8,128,128]{2,1,0:T(8,128)S(1)}, u32[]{:S(2)}, u32[]{:S(2)}) async-start(f32[8,128,128]{2,1,0:T(8,128)} %bitcast.58), calls=%async_computation | async-start | bytes 1048576 | tf_op jit(solution)/shard_map/all_to_all | solution.py:73
  10.5 1.0 %broadcast_multiply_fusion = (f32[1,8192]{1,0:T(1,128)S(1)}, f32[1,8192]{1,0:T(1,128)S(1)}) fusion(f32[64,8192]{1,0:T(8,128)} %param.7, s32[]{:T(128)S(6)} %select_n.47), kind=kLoop, calls=%fused_computation.18 | loop fusion | flops 8192 | bytes 98308 | tf_op jit(solution)/shard_map/mul | solution.py:102
  11.5 2.2 %collective-permute-start.2 = (f32[64,128]{1,0:T(8,128)S(1)}, f32[64,128]{1,0:T(8,128)S(1)}, u32[]{:S(2)}, u32[]{:S(2)}) collective-permute-start(f32[64,128]{1,0:T(8,128)S(1)} %bitcast.63), channel_id=1, source_target_pairs={{0,64},{32,96},{64,0},{96,32},{128,192},{160,224},{192,128},{224,1... | collective-permute-start | bytes 98312 | tf_op jit(solution)/shard_map/ppermute | solution.py:72
  13.8 0.9 %fusion.1 = f32[16]{0:T(128)S(1)} fusion(s32[16]{0:T(128)} %param.8), kind=kOutput, calls=%fused_computation.3 | convolution fusion | flops 3120 | bytes 128 | tf_op jit(solution)/shard_map/dot_general | solution.py:62
  14.6 0.1 reshape.62
  14.7 0.1 mul.90
  14.8 0.9 %dynamic-slice_bitcast_fusion = f32[128,128]{1,0:T(8,128)S(1)} fusion(f32[8,128,128]{2,1,0:T(8,128)} %bitcast.57, s32[]{:T(128)S(6)} %select_n.43), kind=kLoop, calls=%fused_computation.13 | loop fusion | bytes 131076 | tf_op jit(solution)/shard_map/sub | solution.py:77
  15.7 1.3 %all-to-all-done = f32[8,128,128]{2,1,0:T(8,128)S(1)} async-done(((f32[8,128,128]{2,1,0:T(8,128)}), f32[8,128,128]{2,1,0:T(8,128)S(1)}, u32[]{:S(2)}, u32[]{:S(2)}) %all-to-all-start) | async-done | bytes 524320 | tf_op jit(solution)/shard_map/all_to_all | solution.py:73
  17.0 0.1 multiply_reduce_fusion
  17.1 3.2 %collective-permute-start = (f32[128,128]{1,0:T(8,128)S(1)}, f32[128,128]{1,0:T(8,128)S(1)}, u32[]{:S(2)}, u32[]{:S(2)}) collective-permute-start(f32[128,128]{1,0:T(8,128)S(1)} %multiply_reduce_fusion), channel_id=1, source_target_pairs={{0,64},{32,96},{64,0},{96,32},{128,192},{160,224},{192,128},{224,1... | collective-permute-start | bytes 196616 | tf_op jit(solution)/shard_map/ppermute | solution.py:78
  20.3 0.0 collective-permute-done.2
  20.4 3.4 %collective-permute-start.3 = (f32[128,128]{1,0:T(8,128)S(1)}, f32[128,128]{1,0:T(8,128)S(1)}, u32[]{:S(2)}, u32[]{:S(2)}) collective-permute-start(f32[128,128]{1,0:T(8,128)S(1)} %bitcast.60), channel_id=1, source_target_pairs={{0,32},{32,0},{64,96},{96,64},{128,160},{160,128},{192,224},{224,1... | collective-permute-start | bytes 196616 | tf_op jit(solution)/shard_map/ppermute | solution.py:82
  23.8 1.1 %collective-permute-done = f32[128,128]{1,0:T(8,128)S(1)} collective-permute-done((f32[128,128]{1,0:T(8,128)S(1)}, f32[128,128]{1,0:T(8,128)S(1)}, u32[]{:S(2)}, u32[]{:S(2)}) %collective-permute-start) | collective-permute-done | bytes 65568 | tf_op jit(solution)/shard_map/ppermute | solution.py:78
  24.9 0.1 compare_select_fusion
  25.0 0.7 broadcast_in_dim.32
  25.7 7.2 %all-to-all-start.1 = ((f32[64,1,128]{2,1,0:T(1,128)}), f32[64,1,128]{2,1,0:T(1,128)S(1)}, u32[]{:S(2)}, u32[]{:S(2)}) async-start(f32[64,1,128]{2,1,0:T(1,128)} %broadcast_in_dim.32), calls=%async_computation.1 | async-start | bytes 65536 | tf_op jit(solution)/shard_map/all_to_all | solution.py:87
  32.9 3.4 %collective-permute-start.1 = (f32[128,128]{1,0:T(8,128)S(1)}, f32[128,128]{1,0:T(8,128)S(1)}, u32[]{:S(2)}, u32[]{:S(2)}) collective-permute-start(f32[128,128]{1,0:T(8,128)S(1)} %get-tuple-element.15), channel_id=1, source_target_pairs={{0,32},{32,0},{64,96},{96,64},{128,160},{160,128},{192,224},{224,1... | collective-permute-start | bytes 196616 | tf_op jit(solution)/shard_map/ppermute | solution.py:86
  36.3 0.0 collective-permute-done.3
  36.3 3.5 %all-to-all-done.1 = f32[64,1,128]{2,1,0:T(1,128)S(1)} async-done(((f32[64,1,128]{2,1,0:T(1,128)}), f32[64,1,128]{2,1,0:T(1,128)S(1)}, u32[]{:S(2)}, u32[]{:S(2)}) %all-to-all-start.1) | async-done | bytes 32800 | tf_op jit(solution)/shard_map/all_to_all | solution.py:87
  39.9 0.0 collective-permute-done.1
  39.9 1.1 %broadcast_in_dim.34 = f32[4,2,256,128]{3,2,1,0:T(8,128)} broadcast(f32[2,256,128]{2,1,0:T(8,128)S(1)} %pad_maximum_fusion), dimensions={1,2,3} | broadcast | bytes 1310720 | tf_op jit(solution)/shard_map/broadcast_in_dim | solution.py:95
  41.0 4.9 %all-to-all-start.2 = ((f32[4,2,256,128]{3,2,1,0:T(8,128)}), f32[4,2,256,128]{3,2,1,0:T(8,128)S(1)}, u32[]{:S(2)}, u32[]{:S(2)}) async-start(f32[4,2,256,128]{3,2,1,0:T(8,128)} %broadcast_in_dim.34), calls=%async_computation.2 | async-start | bytes 2097152 | tf_op jit(solution)/shard_map/all_to_all | solution.py:96
  45.9 0.0 copy-start
  45.9 18.9 %psum.7 = f32[1,128]{1,0:T(1,128)S(1)} all-reduce(f32[1,128]{1,0:T(1,128)S(1)} %bitcast.69), channel_id=1, replica_groups={{0,2,4,6},{1,3,5,7},{8,10,12,14},{9,11,13,15},{16,18,20,22},{17,19,21,2..., use_global_device_ids=true, to_apply=%region_3.4 | all-reduce | flops 128 | bytes 1024 | tf_op jit(solution)/shard_map/psum | solution.py:98
  64.7 0.0 all-to-all-done.2
  64.7 0.1 fusion.11
  64.9 0.0 copy-done
  64.9 0.9 %multiply_subtract_fusion = f32[131072]{0:T(1024)} fusion(f32[131072]{0:T(1024)S(1)} %copy-done, f32[131072]{0:T(1024)S(1)} %bitcast.54, f32[131072]{0:T(1024)S(1)} %bitcast.52, f32[131072]{0:T(1024)S(1)} %bitcast.55), kind=kLoop, calls=%fused_computation.5 | loop fusion | flops 786432 | bytes 2621440 | tf_op jit(solution)/shard_map/sub | solution.py:106
  65.8 0.6 fusion.2
  (12 shorter events, 0.3 us)
Async XLA Ops:
  0.6 16.4 %all-to-all-start = ((f32[8,128,128]{2,1,0:T(8,128)}), f32[8,128,128]{2,1,0:T(8,128)S(1)}, u32[]{:S(2)}, u32[]{:S(2)}) async-start(f32[8,128,128]{2,1,0:T(8,128)} %bitcast.58), calls=%async_computation | async-start | bytes 1048576 | tf_op jit(solution)/shard_map/all_to_all | solution.py:73
  11.5 8.8 %collective-permute-start.2 = (f32[64,128]{1,0:T(8,128)S(1)}, f32[64,128]{1,0:T(8,128)S(1)}, u32[]{:S(2)}, u32[]{:S(2)}) collective-permute-start(f32[64,128]{1,0:T(8,128)S(1)} %bitcast.63), channel_id=1, source_target_pairs={{0,64},{32,96},{64,0},{96,32},{128,192},{160,224},{192,128},{224,1... | collective-permute-start | bytes 98312 | tf_op jit(solution)/shard_map/ppermute | solution.py:72
  17.1 7.8 %collective-permute-start = (f32[128,128]{1,0:T(8,128)S(1)}, f32[128,128]{1,0:T(8,128)S(1)}, u32[]{:S(2)}, u32[]{:S(2)}) collective-permute-start(f32[128,128]{1,0:T(8,128)S(1)} %multiply_reduce_fusion), channel_id=1, source_target_pairs={{0,64},{32,96},{64,0},{96,32},{128,192},{160,224},{192,128},{224,1... | collective-permute-start | bytes 196616 | tf_op jit(solution)/shard_map/ppermute | solution.py:78
  20.4 15.9 %collective-permute-start.3 = (f32[128,128]{1,0:T(8,128)S(1)}, f32[128,128]{1,0:T(8,128)S(1)}, u32[]{:S(2)}, u32[]{:S(2)}) collective-permute-start(f32[128,128]{1,0:T(8,128)S(1)} %bitcast.60), channel_id=1, source_target_pairs={{0,32},{32,0},{64,96},{96,64},{128,160},{160,128},{192,224},{224,1... | collective-permute-start | bytes 196616 | tf_op jit(solution)/shard_map/ppermute | solution.py:82
  25.7 14.1 %all-to-all-start.1 = ((f32[64,1,128]{2,1,0:T(1,128)}), f32[64,1,128]{2,1,0:T(1,128)S(1)}, u32[]{:S(2)}, u32[]{:S(2)}) async-start(f32[64,1,128]{2,1,0:T(1,128)} %broadcast_in_dim.32), calls=%async_computation.1 | async-start | bytes 65536 | tf_op jit(solution)/shard_map/all_to_all | solution.py:87
  32.9 7.0 %collective-permute-start.1 = (f32[128,128]{1,0:T(8,128)S(1)}, f32[128,128]{1,0:T(8,128)S(1)}, u32[]{:S(2)}, u32[]{:S(2)}) collective-permute-start(f32[128,128]{1,0:T(8,128)S(1)} %get-tuple-element.15), channel_id=1, source_target_pairs={{0,32},{32,0},{64,96},{96,64},{128,160},{160,128},{192,224},{224,1... | collective-permute-start | bytes 196616 | tf_op jit(solution)/shard_map/ppermute | solution.py:86
  41.0 23.7 %all-to-all-start.2 = ((f32[4,2,256,128]{3,2,1,0:T(8,128)}), f32[4,2,256,128]{3,2,1,0:T(8,128)S(1)}, u32[]{:S(2)}, u32[]{:S(2)}) async-start(f32[4,2,256,128]{3,2,1,0:T(8,128)} %broadcast_in_dim.34), calls=%async_computation.2 | async-start | bytes 2097152 | tf_op jit(solution)/shard_map/all_to_all | solution.py:96
  45.9 19.1 %copy-start = (f32[131072]{0:T(1024)S(1)}, f32[131072]{0:T(1024)}, u32[]{:S(2)}) copy-start(f32[131072]{0:T(1024)} %param.5) | copy-start | bytes 1572868

commit v8 on v7

--- a/solution.py
+++ b/solution.py
@@ -1,8 +1,11 @@
+import functools
 import math
 
 import jax
 import jax.numpy as jnp
 from jax import lax
+from jax.experimental import pallas as pl
+from jax.experimental.pallas import tpu as pltpu
 from jax.sharding import PartitionSpec as P
 
 beta_outer = 0.9
@@ -42,6 +45,31 @@
     ones = jnp.ones((lanes, lanes), jnp.float32)
     total = jnp.dot(row * 2.0**-40, ones, precision=lax.Precision.HIGHEST) * 2.0**40
     return jnp.where(jnp.isnan(total), jnp.inf, total)
+
+
+def finish_kernel(
+    limit, squares_ref, old_ref, parts_ref, own_ref, state_ref,
+    new_ref, momentum_ref, new_buffer, momentum_buffer, new_sems, momentum_sem,
+):
+    depth = parts_ref.shape[1] // 2
+    piece = depth // 2
+    scale = jnp.minimum(1.0, limit / jnp.sqrt(squares_ref[...] + epsilon))
+    momentum_buffer[...] = beta_outer * state_ref[...] + own_ref[...] * scale
+    copies = [pltpu.make_async_copy(momentum_buffer, momentum_ref, momentum_sem)]
+    copies[0].start()
+    for y in range(4):
+        for half in range(2):
+            for side in range(2):
+                clipped = parts_ref[y * 2 + half, side * piece : (side + 1) * piece] * scale
+                state = parts_ref[y * 2 + side, depth + half * piece : depth + (half + 1) * piece]
+                start = (y * 4 + half * 2 + side) * piece
+                step = beta_outer * (beta_outer * state + clipped) + clipped
+                new_buffer[start : start + piece] = old_ref[start : start + piece] - rate_outer * step
+        chunk = pl.ds(y * 4 * piece, 4 * piece)
+        copies.append(pltpu.make_async_copy(new_buffer.at[chunk], new_ref.at[chunk], new_sems.at[y]))
+        copies[-1].start()
+    for copy in copies:
+        copy.wait()
 
 
 def local(
@@ -96,14 +124,25 @@
     parts = lax.all_to_all(sent, "replica", 0, 0, axis_index_groups=line_groups(), tiled=True)
     parts = parts.reshape(8, -1, lanes)
     squares = lax.psum(squares, "fsdp", axis_index_groups=far_groups())
-    scale = jnp.minimum(1.0, limit / jnp.sqrt(squares + epsilon))
-    pieces = parts[:, :depth].reshape(replicas, -1, lanes)
-    own = lax.dynamic_index_in_dim(pieces, replica_pos, 0, keepdims=False)
-    new_momentum = beta_outer * state_piece + own * scale
-    clipped = pieces * scale
-    all_state = parts[:, depth:].reshape(4, 2, 2, -1, lanes).swapaxes(1, 2).reshape(pieces.shape)
-    step = beta_outer * (beta_outer * all_state + clipped) + clipped
-    new_weights = blocks.reshape(pieces.shape) - rate_outer * step
+    own = lax.dynamic_slice_in_dim(averages.reshape(-1, lanes), (replica_pos & 3) * (depth // 2), depth // 2)
+    near_by = functools.partial(pltpu.with_memory_space_constraint, memory_space=pltpu.VMEM)
+    vmem = pl.BlockSpec(memory_space=pltpu.VMEM)
+    new_weights, new_momentum = pl.pallas_call(
+        functools.partial(finish_kernel, limit),
+        out_shape=(
+            jax.ShapeDtypeStruct((8 * depth, lanes), jnp.float32),
+            jax.ShapeDtypeStruct(state_piece.shape, jnp.float32),
+        ),
+        in_specs=[vmem] * 5,
+        out_specs=(pl.BlockSpec(memory_space=pl.ANY), pl.BlockSpec(memory_space=pl.ANY)),
+        scratch_shapes=[
+            pltpu.VMEM((8 * depth, lanes), jnp.float32),
+            pltpu.VMEM(state_piece.shape, jnp.float32),
+            pltpu.SemaphoreType.DMA((4,)),
+            pltpu.SemaphoreType.DMA,
+        ],
+        name="finish",
+    )(near_by(squares), near_by(blocks.reshape(-1, lanes)), near_by(parts), near_by(own), near_by(state_piece))
     return (new_weights.reshape(-1), new_momentum.reshape(-1))
 
 

time: 67 us -> 66 us (0.985)
  other arithmetic: 2.87 us -> 0.25 us
  local copies, waits for them, and re-layouts: 2.85 us -> 3.76 us
  Pallas kernels: 0 us -> 0.89 us
    mul x2 -> x0, other arithmetic: 1.01 us -> none  [the longest x1 1 us: local(): new_momentum = beta_outer * state_piece + own * scale]
    dynamic_slice x0 -> x2, local copies, waits for them, and re-layouts: none -> 0.98 us  [the longest x1 0.98 us: local(): lax.dynamic_index_in_dim(momentum, target_fragment_index[0], 0, keepdims=...]
    sub x1 -> x0, other arithmetic: 0.9 us -> none  [local(): new_weights = blocks.reshape(pieces.shape) - rate_outer * step]
    pallas_call x0 -> x1, Pallas kernels: none -> 0.89 us  [local(): pl.pallas_call(functools.partial(finish_kernel, limit), out_shape=(jax.Sh...]
where the time goes in v8:
time: 66 us; the launch traced here: 65.5 us
  starting transfers between devices  33.4 us (51%)
  blocking collectives  18.7 us (28%)
  waiting for transfers between devices  6.01 us (9%)
  local copies, waits for them, and re-layouts  3.76 us (6%)
  between operations  1.44 us (2%)
  matrix products  0.99 us (2%)
  Pallas kernels  0.89 us (1%)
    psum x1, blocking collectives, local(): squares = lax.psum(squares, 'fsdp', axis_index_groups=far_groups())  18.7 us
    all_to_all x1, starting transfers between devices, local(): lax.all_to_all(replica_local_weights[0].reshape(blocks.shape), 'replica',...  9.24 us
    all_to_all x1, starting transfers between devices, local(): lax.all_to_all(squares, ('replica', 'fsdp'), 0, 0, axis_index_groups=near...  7.12 us
    all_to_all x1, starting transfers between devices, local(): lax.all_to_all(sent, 'replica', 0, 0, axis_index_groups=line_groups(), ti...  4.88 us
    all_to_all x1, waiting for transfers between devices, local(): lax.all_to_all(squares, ('replica', 'fsdp'), 0, 0, axis_index_groups=near...  3.51 us
    ppermute x1, starting transfers between devices, local(): lax.ppermute(average, 'replica', [(i, i ^ 1) for i in range(replicas)])  3.41 us
    ppermute x1, starting transfers between devices, local(): lax.ppermute(pair, 'replica', [(i, i ^ 1) for i in range(replicas)])  3.38 us
    ppermute x1, starting transfers between devices, local(): lax.ppermute(partial, 'replica', [(i, i ^ 2) for i in range(replicas)])  3.18 us
  transfers between devices with their start and end apart: 7, of which 3 were waited for; matrix products, arithmetic and copies ran while one was open for 6% of the time, Pallas kernels for 0%

profile of v8, /device:TPU:8, one launch (start us, length us, event | category | flops | bytes accessed | tf_op | source)
XLA Modules:
  0.0 65.5 jit_solution(12374963538353912124)
XLA Ops:
  0.6 9.2 %all-to-all-start = ((f32[8,128,128]{2,1,0:T(8,128)}), f32[8,128,128]{2,1,0:T(8,128)S(1)}, u32[]{:S(2)}, u32[]{:S(2)}) async-start(f32[8,128,128]{2,1,0:T(8,128)} %bitcast.46), calls=%async_computation | async-start | bytes 1048576 | tf_op jit(solution)/shard_map/all_to_all | solution.py:101
  10.5 1.0 %constant_dynamic-slice_fusion.1 = f32[1,8192]{1,0:T(1,128)S(1)} fusion(f32[64,8192]{1,0:T(8,128)} %param.7, s32[]{:T(128)S(6)} %select_n.50), kind=kLoop, calls=%fused_computation.18 | loop fusion | bytes 65540 | tf_op jit(solution)/shard_map/jit(dynamic_index_in_dim)/dynamic_slice | solution.py:95
  11.5 2.2 %collective-permute-start.2 = (f32[64,128]{1,0:T(8,128)S(1)}, f32[64,128]{1,0:T(8,128)S(1)}, u32[]{:S(2)}, u32[]{:S(2)}) collective-permute-start(f32[64,128]{1,0:T(8,128)S(1)} %bitcast.42), channel_id=1, source_target_pairs={{0,64},{32,96},{64,0},{96,32},{128,192},{160,224},{192,128},{224,1... | collective-permute-start | bytes 98312 | tf_op jit(solution)/shard_map/ppermute | solution.py:100
  13.7 0.9 %fusion.1 = f32[16]{0:T(128)S(1)} fusion(s32[16]{0:T(128)} %param.8), kind=kOutput, calls=%fused_computation.3 | convolution fusion | flops 3120 | bytes 128 | tf_op jit(solution)/shard_map/dot_general | solution.py:90
  14.6 0.1 reshape.51
  14.7 0.1 mul.35
  14.8 0.9 %dynamic-slice_bitcast_fusion = f32[128,128]{1,0:T(8,128)S(1)} fusion(f32[8,128,128]{2,1,0:T(8,128)} %bitcast.40, s32[]{:T(128)S(6)} %select_n.46), kind=kLoop, calls=%fused_computation.11 | loop fusion | bytes 131076 | tf_op jit(solution)/shard_map/sub | solution.py:105
  15.7 1.3 %all-to-all-done = f32[8,128,128]{2,1,0:T(8,128)S(1)} async-done(((f32[8,128,128]{2,1,0:T(8,128)}), f32[8,128,128]{2,1,0:T(8,128)S(1)}, u32[]{:S(2)}, u32[]{:S(2)}) %all-to-all-start) | async-done | bytes 524320 | tf_op jit(solution)/shard_map/all_to_all | solution.py:101
  17.0 0.1 multiply_reduce_fusion
  17.1 3.2 %collective-permute-start = (f32[128,128]{1,0:T(8,128)S(1)}, f32[128,128]{1,0:T(8,128)S(1)}, u32[]{:S(2)}, u32[]{:S(2)}) collective-permute-start(f32[128,128]{1,0:T(8,128)S(1)} %multiply_reduce_fusion), channel_id=1, source_target_pairs={{0,64},{32,96},{64,0},{96,32},{128,192},{160,224},{192,128},{224,1... | collective-permute-start | bytes 196616 | tf_op jit(solution)/shard_map/ppermute | solution.py:106
  20.3 0.0 collective-permute-done.2
  20.4 3.4 %collective-permute-start.3 = (f32[128,128]{1,0:T(8,128)S(1)}, f32[128,128]{1,0:T(8,128)S(1)}, u32[]{:S(2)}, u32[]{:S(2)}) collective-permute-start(f32[128,128]{1,0:T(8,128)S(1)} %bitcast.48), channel_id=1, source_target_pairs={{0,32},{32,0},{64,96},{96,64},{128,160},{160,128},{192,224},{224,1... | collective-permute-start | bytes 196616 | tf_op jit(solution)/shard_map/ppermute | solution.py:110
  23.7 1.1 %collective-permute-done = f32[128,128]{1,0:T(8,128)S(1)} collective-permute-done((f32[128,128]{1,0:T(8,128)S(1)}, f32[128,128]{1,0:T(8,128)S(1)}, u32[]{:S(2)}, u32[]{:S(2)}) %collective-permute-start) | collective-permute-done | bytes 65568 | tf_op jit(solution)/shard_map/ppermute | solution.py:106
  24.9 0.1 compare_select_fusion
  25.1 0.7 %broadcast_in_dim.31 = f32[64,1,128]{2,1,0:T(1,128)} broadcast(f32[128]{0:T(128)S(1)} %compare_select_fusion), dimensions={2} | broadcast | bytes 33280 | tf_op jit(solution)/shard_map/broadcast_in_dim | solution.py:113
  25.7 7.1 %all-to-all-start.1 = ((f32[64,1,128]{2,1,0:T(1,128)}), f32[64,1,128]{2,1,0:T(1,128)S(1)}, u32[]{:S(2)}, u32[]{:S(2)}) async-start(f32[64,1,128]{2,1,0:T(1,128)} %broadcast_in_dim.31), calls=%async_computation.1 | async-start | bytes 65536 | tf_op jit(solution)/shard_map/all_to_all | solution.py:115
  32.9 3.4 %collective-permute-start.1 = (f32[128,128]{1,0:T(8,128)S(1)}, f32[128,128]{1,0:T(8,128)S(1)}, u32[]{:S(2)}, u32[]{:S(2)}) collective-permute-start(f32[128,128]{1,0:T(8,128)S(1)} %get-tuple-element.17), channel_id=1, source_target_pairs={{0,32},{32,0},{64,96},{96,64},{128,160},{160,128},{192,224},{224,1... | collective-permute-start | bytes 196616 | tf_op jit(solution)/shard_map/ppermute | solution.py:114
  36.3 0.0 collective-permute-done.3
  36.3 3.5 %all-to-all-done.1 = f32[64,1,128]{2,1,0:T(1,128)S(1)} async-done(((f32[64,1,128]{2,1,0:T(1,128)}), f32[64,1,128]{2,1,0:T(1,128)S(1)}, u32[]{:S(2)}, u32[]{:S(2)}) %all-to-all-start.1) | async-done | bytes 32800 | tf_op jit(solution)/shard_map/all_to_all | solution.py:115
  39.9 0.0 collective-permute-done.1
  39.9 0.0 copy-start
  39.9 1.1 %broadcast_in_dim.33 = f32[4,2,256,128]{3,2,1,0:T(8,128)} broadcast(f32[2,256,128]{2,1,0:T(8,128)S(1)} %pad_maximum_fusion), dimensions={1,2,3} | broadcast | bytes 1310720 | tf_op jit(solution)/shard_map/broadcast_in_dim | solution.py:123
  41.0 4.9 %all-to-all-start.2 = ((f32[4,2,256,128]{3,2,1,0:T(8,128)}), f32[4,2,256,128]{3,2,1,0:T(8,128)S(1)}, u32[]{:S(2)}, u32[]{:S(2)}) async-start(f32[4,2,256,128]{3,2,1,0:T(8,128)} %broadcast_in_dim.33), calls=%async_computation.2 | async-start | bytes 2097152 | tf_op jit(solution)/shard_map/all_to_all | solution.py:124
  45.9 18.7 %psum.7.squares_ref = f32[1,128]{1,0:T(1,128)S(1)} all-reduce(f32[1,128]{1,0:T(1,128)S(1)} %bitcast.54), channel_id=1, replica_groups={{0,2,4,6},{1,3,5,7},{8,10,12,14},{9,11,13,15},{16,18,20,22},{17,19,21,2..., use_global_device_ids=true, to_apply=%region_3.4 | all-reduce | flops 128 | bytes 1024 | tf_op jit(solution)/shard_map/psum | solution.py:126
  64.6 0.0 all-to-all-done.2
  64.6 0.0 copy-done
  64.6 0.9 %finish.1 = (f32[1024,128]{1,0:T(8,128)}, f32[64,128]{1,0:T(8,128)}) custom-call(f32[1,128]{1,0:T(1,128)S(1)} %psum.7.squares_ref, f32[1024,128]{1,0:T(8,128)S(1)} %bitcast.41, f32[8,256,128]{2,1,0:T(8,128)S(1)} %bitcast.39, f32[64,128]{1,0:T(8,128)S(1)} %constant_dynamic-slice_fusion.own_ref, f32[64,128]{1,0:T(8,128)S(1)} %bitcast.44), custom_call_target="tpu_custom_call" | custom-call | tf_op jit(solution)/shard_map/finish/pallas_call | solution.py:130
  (10 shorter events, 0.2 us)
Async XLA Ops:
  0.6 16.4 %all-to-all-start = ((f32[8,128,128]{2,1,0:T(8,128)}), f32[8,128,128]{2,1,0:T(8,128)S(1)}, u32[]{:S(2)}, u32[]{:S(2)}) async-start(f32[8,128,128]{2,1,0:T(8,128)} %bitcast.46), calls=%async_computation | async-start | bytes 1048576 | tf_op jit(solution)/shard_map/all_to_all | solution.py:101
  11.5 8.8 %collective-permute-start.2 = (f32[64,128]{1,0:T(8,128)S(1)}, f32[64,128]{1,0:T(8,128)S(1)}, u32[]{:S(2)}, u32[]{:S(2)}) collective-permute-start(f32[64,128]{1,0:T(8,128)S(1)} %bitcast.42), channel_id=1, source_target_pairs={{0,64},{32,96},{64,0},{96,32},{128,192},{160,224},{192,128},{224,1... | collective-permute-start | bytes 98312 | tf_op jit(solution)/shard_map/ppermute | solution.py:100
  17.1 7.8 %collective-permute-start = (f32[128,128]{1,0:T(8,128)S(1)}, f32[128,128]{1,0:T(8,128)S(1)}, u32[]{:S(2)}, u32[]{:S(2)}) collective-permute-start(f32[128,128]{1,0:T(8,128)S(1)} %multiply_reduce_fusion), channel_id=1, source_target_pairs={{0,64},{32,96},{64,0},{96,32},{128,192},{160,224},{192,128},{224,1... | collective-permute-start | bytes 196616 | tf_op jit(solution)/shard_map/ppermute | solution.py:106
  20.4 15.9 %collective-permute-start.3 = (f32[128,128]{1,0:T(8,128)S(1)}, f32[128,128]{1,0:T(8,128)S(1)}, u32[]{:S(2)}, u32[]{:S(2)}) collective-permute-start(f32[128,128]{1,0:T(8,128)S(1)} %bitcast.48), channel_id=1, source_target_pairs={{0,32},{32,0},{64,96},{96,64},{128,160},{160,128},{192,224},{224,1... | collective-permute-start | bytes 196616 | tf_op jit(solution)/shard_map/ppermute | solution.py:110
  25.7 14.1 %all-to-all-start.1 = ((f32[64,1,128]{2,1,0:T(1,128)}), f32[64,1,128]{2,1,0:T(1,128)S(1)}, u32[]{:S(2)}, u32[]{:S(2)}) async-start(f32[64,1,128]{2,1,0:T(1,128)} %broadcast_in_dim.31), calls=%async_computation.1 | async-start | bytes 65536 | tf_op jit(solution)/shard_map/all_to_all | solution.py:115
  32.9 7.0 %collective-permute-start.1 = (f32[128,128]{1,0:T(8,128)S(1)}, f32[128,128]{1,0:T(8,128)S(1)}, u32[]{:S(2)}, u32[]{:S(2)}) collective-permute-start(f32[128,128]{1,0:T(8,128)S(1)} %get-tuple-element.17), channel_id=1, source_target_pairs={{0,32},{32,0},{64,96},{96,64},{128,160},{160,128},{192,224},{224,1... | collective-permute-start | bytes 196616 | tf_op jit(solution)/shard_map/ppermute | solution.py:114
  39.9 24.8 %copy-start = (f32[131072]{0:T(1024)S(1)}, f32[131072]{0:T(1024)}, u32[]{:S(2)}) copy-start(f32[131072]{0:T(1024)} %param.5) | copy-start | bytes 1572868
  41.0 23.6 %all-to-all-start.2 = ((f32[4,2,256,128]{3,2,1,0:T(8,128)}), f32[4,2,256,128]{3,2,1,0:T(8,128)S(1)}, u32[]{:S(2)}, u32[]{:S(2)}) async-start(f32[4,2,256,128]{3,2,1,0:T(8,128)} %broadcast_in_dim.33), calls=%async_computation.2 | async-start | bytes 2097152 | tf_op jit(solution)/shard_map/all_to_all | solution.py:124

commit v9 on v8

--- a/solution.py
+++ b/solution.py
@@ -41,19 +41,13 @@
     return [[x * 8 + far * 2 + core for far in range(4)] for x in range(4) for core in range(2)]
 
 
-def lane_total(row):
-    ones = jnp.ones((lanes, lanes), jnp.float32)
-    total = jnp.dot(row * 2.0**-40, ones, precision=lax.Precision.HIGHEST) * 2.0**40
-    return jnp.where(jnp.isnan(total), jnp.inf, total)
-
-
 def finish_kernel(
     limit, squares_ref, old_ref, parts_ref, own_ref, state_ref,
     new_ref, momentum_ref, new_buffer, momentum_buffer, new_sems, momentum_sem,
 ):
     depth = parts_ref.shape[1] // 2
     piece = depth // 2
-    scale = jnp.minimum(1.0, limit / jnp.sqrt(squares_ref[...] + epsilon))
+    scale = jnp.minimum(1.0, limit / jnp.sqrt(jnp.sum(squares_ref[...], keepdims=True) + epsilon))
     momentum_buffer[...] = beta_outer * state_ref[...] + own_ref[...] * scale
     copies = [pltpu.make_async_copy(momentum_buffer, momentum_ref, momentum_sem)]
     copies[0].start()
@@ -109,11 +103,11 @@
     pair = jnp.where(half == 0, pair, pair[::-1]).reshape(depth, lanes)
     beside_pair = lax.ppermute(pair, "replica", [(i, i ^ 1) for i in range(replicas)])
     near = near_groups(shards)
-    squares = lane_total(jnp.sum(average * average, 0, keepdims=True))
+    squares = jnp.sum(average * average, 0, keepdims=True)
     squares = jnp.broadcast_to(squares[None], (len(near[0]), 1, lanes))
     beside = lax.ppermute(average, "replica", [(i, i ^ 1) for i in range(replicas)])
     squares = lax.all_to_all(squares, ("replica", "fsdp"), 0, 0, axis_index_groups=near, tiled=True)
-    squares = jnp.sum(squares[:32, 0] + squares[32:, 0], 0, keepdims=True)
+    squares = jnp.sum((squares[:32, 0] + squares[32:, 0]).reshape(4, 8, lanes), 0)
     beside, squares = lax.optimization_barrier((beside, squares))
     first = side == 0
     averages = jnp.where(first, jnp.stack([average, beside]), jnp.stack([beside, average]))

time: 66 us -> 66 us (level)
  no operation moved by 1% of the time
where the time goes in v9:
time: 66 us; the launch traced here: 65.5 us
  starting transfers between devices  33.4 us (51%)
  blocking collectives  18.7 us (28%)
  waiting for transfers between devices  6.01 us (9%)
  local copies, waits for them, and re-layouts  3.74 us (6%)
  between operations  1.46 us (2%)
  Pallas kernels  1.01 us (2%)
  matrix products  0.86 us (1%)
    psum x1, blocking collectives, local(): squares = lax.psum(squares, 'fsdp', axis_index_groups=far_groups())  18.7 us
    all_to_all x1, starting transfers between devices, local(): lax.all_to_all(replica_local_weights[0].reshape(blocks.shape), 'replica',...  9.24 us
    all_to_all x1, starting transfers between devices, local(): lax.all_to_all(squares, ('replica', 'fsdp'), 0, 0, axis_index_groups=near...  7.12 us
    all_to_all x1, starting transfers between devices, local(): lax.all_to_all(sent, 'replica', 0, 0, axis_index_groups=line_groups(), ti...  4.88 us
    all_to_all x1, waiting for transfers between devices, local(): lax.all_to_all(squares, ('replica', 'fsdp'), 0, 0, axis_index_groups=near...  3.51 us
    ppermute x1, starting transfers between devices, local(): lax.ppermute(average, 'replica', [(i, i ^ 1) for i in range(replicas)])  3.41 us
    ppermute x1, starting transfers between devices, local(): lax.ppermute(pair, 'replica', [(i, i ^ 1) for i in range(replicas)])  3.38 us
    ppermute x1, starting transfers between devices, local(): lax.ppermute(partial, 'replica', [(i, i ^ 2) for i in range(replicas)])  3.18 us
  transfers between devices with their start and end apart: 7, of which 3 were waited for; matrix products, arithmetic and copies ran while one was open for 6% of the time, Pallas kernels for 0%

profile of v9, /device:TPU:8, one launch (start us, length us, event | category | flops | bytes accessed | tf_op | source)
XLA Modules:
  0.0 65.5 jit_solution(4827941933620993020)
XLA Ops:
  0.6 9.2 %all-to-all-start = ((f32[8,128,128]{2,1,0:T(8,128)}), f32[8,128,128]{2,1,0:T(8,128)S(1)}, u32[]{:S(2)}, u32[]{:S(2)}) async-start(f32[8,128,128]{2,1,0:T(8,128)} %bitcast.38), calls=%async_computation | async-start | bytes 1048576 | tf_op jit(solution)/shard_map/all_to_all | solution.py:95
  10.5 1.0 %constant_dynamic-slice_fusion.1 = f32[1,8192]{1,0:T(1,128)S(1)} fusion(f32[64,8192]{1,0:T(8,128)} %param.7, s32[]{:T(128)S(6)} %select_n.44), kind=kLoop, calls=%fused_computation.15 | loop fusion | bytes 65540 | tf_op jit(solution)/shard_map/jit(dynamic_index_in_dim)/dynamic_slice | solution.py:89
  11.5 2.2 %collective-permute-start.2 = (f32[64,128]{1,0:T(8,128)S(1)}, f32[64,128]{1,0:T(8,128)S(1)}, u32[]{:S(2)}, u32[]{:S(2)}) collective-permute-start(f32[64,128]{1,0:T(8,128)S(1)} %bitcast.34), channel_id=1, source_target_pairs={{0,64},{32,96},{64,0},{96,32},{128,192},{160,224},{192,128},{224,1... | collective-permute-start | bytes 98312 | tf_op jit(solution)/shard_map/ppermute | solution.py:94
  13.7 0.9 %fusion = f32[16]{0:T(128)S(1)} fusion(s32[16]{0:T(128)} %param.8), kind=kOutput, calls=%fused_computation.1 | convolution fusion | flops 3120 | bytes 128 | tf_op jit(solution)/shard_map/dot_general | solution.py:84
  14.6 0.1 reshape.46
  14.7 0.1 mul.19
  14.8 0.9 %dynamic-slice_bitcast_fusion = f32[128,128]{1,0:T(8,128)S(1)} fusion(f32[8,128,128]{2,1,0:T(8,128)} %bitcast.32, s32[]{:T(128)S(6)} %select_n.41), kind=kLoop, calls=%fused_computation.9 | loop fusion | bytes 131076 | tf_op jit(solution)/shard_map/sub | solution.py:99
  15.7 1.3 %all-to-all-done = f32[8,128,128]{2,1,0:T(8,128)S(1)} async-done(((f32[8,128,128]{2,1,0:T(8,128)}), f32[8,128,128]{2,1,0:T(8,128)S(1)}, u32[]{:S(2)}, u32[]{:S(2)}) %all-to-all-start) | async-done | bytes 524320 | tf_op jit(solution)/shard_map/all_to_all | solution.py:95
  17.0 0.1 multiply_reduce_fusion
  17.1 3.2 %collective-permute-start = (f32[128,128]{1,0:T(8,128)S(1)}, f32[128,128]{1,0:T(8,128)S(1)}, u32[]{:S(2)}, u32[]{:S(2)}) collective-permute-start(f32[128,128]{1,0:T(8,128)S(1)} %multiply_reduce_fusion), channel_id=1, source_target_pairs={{0,64},{32,96},{64,0},{96,32},{128,192},{160,224},{192,128},{224,1... | collective-permute-start | bytes 196616 | tf_op jit(solution)/shard_map/ppermute | solution.py:100
  20.3 0.0 collective-permute-done.2
  20.4 3.4 %collective-permute-start.3 = (f32[128,128]{1,0:T(8,128)S(1)}, f32[128,128]{1,0:T(8,128)S(1)}, u32[]{:S(2)}, u32[]{:S(2)}) collective-permute-start(f32[128,128]{1,0:T(8,128)S(1)} %bitcast.40), channel_id=1, source_target_pairs={{0,32},{32,0},{64,96},{96,64},{128,160},{160,128},{192,224},{224,1... | collective-permute-start | bytes 196616 | tf_op jit(solution)/shard_map/ppermute | solution.py:104
  23.7 1.1 %collective-permute-done = f32[128,128]{1,0:T(8,128)S(1)} collective-permute-done((f32[128,128]{1,0:T(8,128)S(1)}, f32[128,128]{1,0:T(8,128)S(1)}, u32[]{:S(2)}, u32[]{:S(2)}) %collective-permute-start) | collective-permute-done | bytes 65568 | tf_op jit(solution)/shard_map/ppermute | solution.py:100
  24.9 0.6 broadcast_in_dim.7
  25.6 7.1 %all-to-all-start.1 = ((f32[64,1,128]{2,1,0:T(1,128)}), f32[64,1,128]{2,1,0:T(1,128)S(1)}, u32[]{:S(2)}, u32[]{:S(2)}) async-start(f32[64,1,128]{2,1,0:T(1,128)} %broadcast_in_dim.7), calls=%async_computation.1 | async-start | bytes 65536 | tf_op jit(solution)/shard_map/all_to_all | solution.py:109
  32.7 3.4 %collective-permute-start.1 = (f32[128,128]{1,0:T(8,128)S(1)}, f32[128,128]{1,0:T(8,128)S(1)}, u32[]{:S(2)}, u32[]{:S(2)}) collective-permute-start(f32[128,128]{1,0:T(8,128)S(1)} %get-tuple-element.17), channel_id=1, source_target_pairs={{0,32},{32,0},{64,96},{96,64},{128,160},{160,128},{192,224},{224,1... | collective-permute-start | bytes 196616 | tf_op jit(solution)/shard_map/ppermute | solution.py:108
  36.1 0.0 collective-permute-done.3
  36.1 3.5 %all-to-all-done.1 = f32[64,1,128]{2,1,0:T(1,128)S(1)} async-done(((f32[64,1,128]{2,1,0:T(1,128)}), f32[64,1,128]{2,1,0:T(1,128)S(1)}, u32[]{:S(2)}, u32[]{:S(2)}) %all-to-all-start.1) | async-done | bytes 32800 | tf_op jit(solution)/shard_map/all_to_all | solution.py:109
  39.7 0.0 collective-permute-done.1
  39.7 0.0 copy-start
  39.8 1.1 %broadcast_in_dim.8 = f32[4,2,256,128]{3,2,1,0:T(8,128)} broadcast(f32[2,256,128]{2,1,0:T(8,128)S(1)} %pad_maximum_fusion), dimensions={1,2,3} | broadcast | bytes 1310720 | tf_op jit(solution)/shard_map/broadcast_in_dim | solution.py:117
  40.8 4.9 %all-to-all-start.2 = ((f32[4,2,256,128]{3,2,1,0:T(8,128)}), f32[4,2,256,128]{3,2,1,0:T(8,128)S(1)}, u32[]{:S(2)}, u32[]{:S(2)}) async-start(f32[4,2,256,128]{3,2,1,0:T(8,128)} %broadcast_in_dim.8), calls=%async_computation.2 | async-start | bytes 2097152 | tf_op jit(solution)/shard_map/all_to_all | solution.py:118
  45.7 18.7 %psum.7.squares_ref = f32[8,128]{1,0:T(8,128)S(1)} all-reduce(f32[8,128]{1,0:T(8,128)S(1)} %bitcast_reduce_fusion), channel_id=1, replica_groups={{0,2,4,6},{1,3,5,7},{8,10,12,14},{9,11,13,15},{16,18,20,22},{17,19,21,2..., use_global_device_ids=true, to_apply=%region_3.4 | all-reduce | flops 1024 | bytes 8192 | tf_op jit(solution)/shard_map/psum | solution.py:120
  64.4 0.0 all-to-all-done.2
  64.5 0.0 copy-done
  64.5 1.0 %finish.1 = (f32[1024,128]{1,0:T(8,128)}, f32[64,128]{1,0:T(8,128)}) custom-call(f32[8,128]{1,0:T(8,128)S(1)} %psum.7.squares_ref, f32[1024,128]{1,0:T(8,128)S(1)} %bitcast.33, f32[8,256,128]{2,1,0:T(8,128)S(1)} %bitcast.31, f32[64,128]{1,0:T(8,128)S(1)} %constant_dynamic-slice_fusion.own_ref, f32[64,128]{1,0:T(8,128)S(1)} %bitcast.36), custom_call_target="tpu_custom_call" | custom-call | tf_op jit(solution)/shard_map/finish/pallas_call | solution.py:124
  (10 shorter events, 0.2 us)
Async XLA Ops:
  0.6 16.4 %all-to-all-start = ((f32[8,128,128]{2,1,0:T(8,128)}), f32[8,128,128]{2,1,0:T(8,128)S(1)}, u32[]{:S(2)}, u32[]{:S(2)}) async-start(f32[8,128,128]{2,1,0:T(8,128)} %bitcast.38), calls=%async_computation | async-start | bytes 1048576 | tf_op jit(solution)/shard_map/all_to_all | solution.py:95
  11.5 8.8 %collective-permute-start.2 = (f32[64,128]{1,0:T(8,128)S(1)}, f32[64,128]{1,0:T(8,128)S(1)}, u32[]{:S(2)}, u32[]{:S(2)}) collective-permute-start(f32[64,128]{1,0:T(8,128)S(1)} %bitcast.34), channel_id=1, source_target_pairs={{0,64},{32,96},{64,0},{96,32},{128,192},{160,224},{192,128},{224,1... | collective-permute-start | bytes 98312 | tf_op jit(solution)/shard_map/ppermute | solution.py:94
  17.1 7.8 %collective-permute-start = (f32[128,128]{1,0:T(8,128)S(1)}, f32[128,128]{1,0:T(8,128)S(1)}, u32[]{:S(2)}, u32[]{:S(2)}) collective-permute-start(f32[128,128]{1,0:T(8,128)S(1)} %multiply_reduce_fusion), channel_id=1, source_target_pairs={{0,64},{32,96},{64,0},{96,32},{128,192},{160,224},{192,128},{224,1... | collective-permute-start | bytes 196616 | tf_op jit(solution)/shard_map/ppermute | solution.py:100
  20.4 15.8 %collective-permute-start.3 = (f32[128,128]{1,0:T(8,128)S(1)}, f32[128,128]{1,0:T(8,128)S(1)}, u32[]{:S(2)}, u32[]{:S(2)}) collective-permute-start(f32[128,128]{1,0:T(8,128)S(1)} %bitcast.40), channel_id=1, source_target_pairs={{0,32},{32,0},{64,96},{96,64},{128,160},{160,128},{192,224},{224,1... | collective-permute-start | bytes 196616 | tf_op jit(solution)/shard_map/ppermute | solution.py:104
  25.6 14.1 %all-to-all-start.1 = ((f32[64,1,128]{2,1,0:T(1,128)}), f32[64,1,128]{2,1,0:T(1,128)S(1)}, u32[]{:S(2)}, u32[]{:S(2)}) async-start(f32[64,1,128]{2,1,0:T(1,128)} %broadcast_in_dim.7), calls=%async_computation.1 | async-start | bytes 65536 | tf_op jit(solution)/shard_map/all_to_all | solution.py:109
  32.7 7.0 %collective-permute-start.1 = (f32[128,128]{1,0:T(8,128)S(1)}, f32[128,128]{1,0:T(8,128)S(1)}, u32[]{:S(2)}, u32[]{:S(2)}) collective-permute-start(f32[128,128]{1,0:T(8,128)S(1)} %get-tuple-element.17), channel_id=1, source_target_pairs={{0,32},{32,0},{64,96},{96,64},{128,160},{160,128},{192,224},{224,1... | collective-permute-start | bytes 196616 | tf_op jit(solution)/shard_map/ppermute | solution.py:108
  39.7 24.8 %copy-start = (f32[131072]{0:T(1024)S(1)}, f32[131072]{0:T(1024)}, u32[]{:S(2)}) copy-start(f32[131072]{0:T(1024)} %param.5) | copy-start | bytes 1572868
  40.8 23.6 %all-to-all-start.2 = ((f32[4,2,256,128]{3,2,1,0:T(8,128)}), f32[4,2,256,128]{3,2,1,0:T(8,128)S(1)}, u32[]{:S(2)}, u32[]{:S(2)}) async-start(f32[4,2,256,128]{3,2,1,0:T(8,128)} %broadcast_in_dim.8), calls=%async_computation.2 | async-start | bytes 2097152 | tf_op jit(solution)/shard_map/all_to_all | solution.py:118

commit v10 on v9

--- a/solution.py
+++ b/solution.py
@@ -47,18 +47,24 @@
 ):
     depth = parts_ref.shape[1] // 2
     piece = depth // 2
+    held = rate_outer * beta_outer * beta_outer
+    for y in range(4):
+        for half in range(2):
+            for side in range(2):
+                state = parts_ref[y * 2 + side, depth + half * piece : depth + (half + 1) * piece]
+                start = (y * 4 + half * 2 + side) * piece
+                new_buffer[start : start + piece] = old_ref[start : start + piece] - held * state
     scale = jnp.minimum(1.0, limit / jnp.sqrt(jnp.sum(squares_ref[...], keepdims=True) + epsilon))
+    gain = rate_outer * (beta_outer + 1.0) * scale
     momentum_buffer[...] = beta_outer * state_ref[...] + own_ref[...] * scale
     copies = [pltpu.make_async_copy(momentum_buffer, momentum_ref, momentum_sem)]
     copies[0].start()
     for y in range(4):
         for half in range(2):
             for side in range(2):
-                clipped = parts_ref[y * 2 + half, side * piece : (side + 1) * piece] * scale
-                state = parts_ref[y * 2 + side, depth + half * piece : depth + (half + 1) * piece]
+                average = parts_ref[y * 2 + half, side * piece : (side + 1) * piece]
                 start = (y * 4 + half * 2 + side) * piece
-                step = beta_outer * (beta_outer * state + clipped) + clipped
-                new_buffer[start : start + piece] = old_ref[start : start + piece] - rate_outer * step
+                new_buffer[start : start + piece] = new_buffer[start : start + piece] - gain * average
         chunk = pl.ds(y * 4 * piece, 4 * piece)
         copies.append(pltpu.make_async_copy(new_buffer.at[chunk], new_ref.at[chunk], new_sems.at[y]))
         copies[-1].start()

time: 66 us -> 66 us (level)
  no operation moved by 1% of the time
where the time goes in v10:
time: 66 us; the launch traced here: 65.5 us
  starting transfers between devices  33.4 us (51%)
  blocking collectives  18.7 us (28%)
  waiting for transfers between devices  6.01 us (9%)
  local copies, waits for them, and re-layouts  3.74 us (6%)
  between operations  1.46 us (2%)
  Pallas kernels  1.04 us (2%)
  matrix products  0.86 us (1%)
    psum x1, blocking collectives, local(): squares = lax.psum(squares, 'fsdp', axis_index_groups=far_groups())  18.7 us
    all_to_all x1, starting transfers between devices, local(): lax.all_to_all(replica_local_weights[0].reshape(blocks.shape), 'replica',...  9.24 us
    all_to_all x1, starting transfers between devices, local(): lax.all_to_all(squares, ('replica', 'fsdp'), 0, 0, axis_index_groups=near...  7.12 us
    all_to_all x1, starting transfers between devices, local(): lax.all_to_all(sent, 'replica', 0, 0, axis_index_groups=line_groups(), ti...  4.88 us
    all_to_all x1, waiting for transfers between devices, local(): lax.all_to_all(squares, ('replica', 'fsdp'), 0, 0, axis_index_groups=near...  3.51 us
    ppermute x1, starting transfers between devices, local(): lax.ppermute(average, 'replica', [(i, i ^ 1) for i in range(replicas)])  3.41 us
    ppermute x1, starting transfers between devices, local(): lax.ppermute(pair, 'replica', [(i, i ^ 1) for i in range(replicas)])  3.38 us
    ppermute x1, starting transfers between devices, local(): lax.ppermute(partial, 'replica', [(i, i ^ 2) for i in range(replicas)])  3.18 us
  transfers between devices with their start and end apart: 7, of which 3 were waited for; matrix products, arithmetic and copies ran while one was open for 6% of the time, Pallas kernels for 0%

profile of v10, /device:TPU:8, one launch (start us, length us, event | category | flops | bytes accessed | tf_op | source)
XLA Modules:
  0.0 65.5 jit_solution(9459379158680157461)
XLA Ops:
  0.6 9.2 %all-to-all-start = ((f32[8,128,128]{2,1,0:T(8,128)}), f32[8,128,128]{2,1,0:T(8,128)S(1)}, u32[]{:S(2)}, u32[]{:S(2)}) async-start(f32[8,128,128]{2,1,0:T(8,128)} %bitcast.38), calls=%async_computation | async-start | bytes 1048576 | tf_op jit(solution)/shard_map/all_to_all | solution.py:101
  10.5 1.0 %constant_dynamic-slice_fusion.1 = f32[1,8192]{1,0:T(1,128)S(1)} fusion(f32[64,8192]{1,0:T(8,128)} %param.7, s32[]{:T(128)S(6)} %select_n.44), kind=kLoop, calls=%fused_computation.15 | loop fusion | bytes 65540 | tf_op jit(solution)/shard_map/jit(dynamic_index_in_dim)/dynamic_slice | solution.py:95
  11.5 2.2 %collective-permute-start.2 = (f32[64,128]{1,0:T(8,128)S(1)}, f32[64,128]{1,0:T(8,128)S(1)}, u32[]{:S(2)}, u32[]{:S(2)}) collective-permute-start(f32[64,128]{1,0:T(8,128)S(1)} %bitcast.34), channel_id=1, source_target_pairs={{0,64},{32,96},{64,0},{96,32},{128,192},{160,224},{192,128},{224,1... | collective-permute-start | bytes 98312 | tf_op jit(solution)/shard_map/ppermute | solution.py:100
  13.7 0.9 %fusion = f32[16]{0:T(128)S(1)} fusion(s32[16]{0:T(128)} %param.8), kind=kOutput, calls=%fused_computation.1 | convolution fusion | flops 3120 | bytes 128 | tf_op jit(solution)/shard_map/dot_general | solution.py:90
  14.6 0.1 reshape.46
  14.7 0.1 mul.19
  14.8 0.9 %dynamic-slice_bitcast_fusion = f32[128,128]{1,0:T(8,128)S(1)} fusion(f32[8,128,128]{2,1,0:T(8,128)} %bitcast.32, s32[]{:T(128)S(6)} %select_n.41), kind=kLoop, calls=%fused_computation.9 | loop fusion | bytes 131076 | tf_op jit(solution)/shard_map/sub | solution.py:105
  15.7 1.3 %all-to-all-done = f32[8,128,128]{2,1,0:T(8,128)S(1)} async-done(((f32[8,128,128]{2,1,0:T(8,128)}), f32[8,128,128]{2,1,0:T(8,128)S(1)}, u32[]{:S(2)}, u32[]{:S(2)}) %all-to-all-start) | async-done | bytes 524320 | tf_op jit(solution)/shard_map/all_to_all | solution.py:101
  17.0 0.1 multiply_reduce_fusion
  17.1 3.2 %collective-permute-start = (f32[128,128]{1,0:T(8,128)S(1)}, f32[128,128]{1,0:T(8,128)S(1)}, u32[]{:S(2)}, u32[]{:S(2)}) collective-permute-start(f32[128,128]{1,0:T(8,128)S(1)} %multiply_reduce_fusion), channel_id=1, source_target_pairs={{0,64},{32,96},{64,0},{96,32},{128,192},{160,224},{192,128},{224,1... | collective-permute-start | bytes 196616 | tf_op jit(solution)/shard_map/ppermute | solution.py:106
  20.3 0.0 collective-permute-done.2
  20.4 3.4 %collective-permute-start.3 = (f32[128,128]{1,0:T(8,128)S(1)}, f32[128,128]{1,0:T(8,128)S(1)}, u32[]{:S(2)}, u32[]{:S(2)}) collective-permute-start(f32[128,128]{1,0:T(8,128)S(1)} %bitcast.40), channel_id=1, source_target_pairs={{0,32},{32,0},{64,96},{96,64},{128,160},{160,128},{192,224},{224,1... | collective-permute-start | bytes 196616 | tf_op jit(solution)/shard_map/ppermute | solution.py:110
  23.7 1.1 %collective-permute-done = f32[128,128]{1,0:T(8,128)S(1)} collective-permute-done((f32[128,128]{1,0:T(8,128)S(1)}, f32[128,128]{1,0:T(8,128)S(1)}, u32[]{:S(2)}, u32[]{:S(2)}) %collective-permute-start) | collective-permute-done | bytes 65568 | tf_op jit(solution)/shard_map/ppermute | solution.py:106
  24.9 0.6 broadcast_in_dim.7
  25.6 7.1 %all-to-all-start.1 = ((f32[64,1,128]{2,1,0:T(1,128)}), f32[64,1,128]{2,1,0:T(1,128)S(1)}, u32[]{:S(2)}, u32[]{:S(2)}) async-start(f32[64,1,128]{2,1,0:T(1,128)} %broadcast_in_dim.7), calls=%async_computation.1 | async-start | bytes 65536 | tf_op jit(solution)/shard_map/all_to_all | solution.py:115
  32.7 3.4 %collective-permute-start.1 = (f32[128,128]{1,0:T(8,128)S(1)}, f32[128,128]{1,0:T(8,128)S(1)}, u32[]{:S(2)}, u32[]{:S(2)}) collective-permute-start(f32[128,128]{1,0:T(8,128)S(1)} %get-tuple-element.17), channel_id=1, source_target_pairs={{0,32},{32,0},{64,96},{96,64},{128,160},{160,128},{192,224},{224,1... | collective-permute-start | bytes 196616 | tf_op jit(solution)/shard_map/ppermute | solution.py:114
  36.1 0.0 collective-permute-done.3
  36.1 3.5 %all-to-all-done.1 = f32[64,1,128]{2,1,0:T(1,128)S(1)} async-done(((f32[64,1,128]{2,1,0:T(1,128)}), f32[64,1,128]{2,1,0:T(1,128)S(1)}, u32[]{:S(2)}, u32[]{:S(2)}) %all-to-all-start.1) | async-done | bytes 32800 | tf_op jit(solution)/shard_map/all_to_all | solution.py:115
  39.7 0.0 collective-permute-done.1
  39.7 0.0 copy-start
  39.8 1.1 %broadcast_in_dim.8 = f32[4,2,256,128]{3,2,1,0:T(8,128)} broadcast(f32[2,256,128]{2,1,0:T(8,128)S(1)} %pad_maximum_fusion), dimensions={1,2,3} | broadcast | bytes 1310720 | tf_op jit(solution)/shard_map/broadcast_in_dim | solution.py:123
  40.8 4.9 %all-to-all-start.2 = ((f32[4,2,256,128]{3,2,1,0:T(8,128)}), f32[4,2,256,128]{3,2,1,0:T(8,128)S(1)}, u32[]{:S(2)}, u32[]{:S(2)}) async-start(f32[4,2,256,128]{3,2,1,0:T(8,128)} %broadcast_in_dim.8), calls=%async_computation.2 | async-start | bytes 2097152 | tf_op jit(solution)/shard_map/all_to_all | solution.py:124
  45.7 18.7 %psum.7.squares_ref = f32[8,128]{1,0:T(8,128)S(1)} all-reduce(f32[8,128]{1,0:T(8,128)S(1)} %bitcast_reduce_fusion), channel_id=1, replica_groups={{0,2,4,6},{1,3,5,7},{8,10,12,14},{9,11,13,15},{16,18,20,22},{17,19,21,2..., use_global_device_ids=true, to_apply=%region_3.4 | all-reduce | flops 1024 | bytes 8192 | tf_op jit(solution)/shard_map/psum | solution.py:126
  64.4 0.0 all-to-all-done.2
  64.5 0.0 copy-done
  64.5 1.0 %finish.1 = (f32[1024,128]{1,0:T(8,128)}, f32[64,128]{1,0:T(8,128)}) custom-call(f32[8,128]{1,0:T(8,128)S(1)} %psum.7.squares_ref, f32[1024,128]{1,0:T(8,128)S(1)} %bitcast.33, f32[8,256,128]{2,1,0:T(8,128)S(1)} %bitcast.31, f32[64,128]{1,0:T(8,128)S(1)} %constant_dynamic-slice_fusion.own_ref, f32[64,128]{1,0:T(8,128)S(1)} %bitcast.36), custom_call_target="tpu_custom_call" | custom-call | tf_op jit(solution)/shard_map/finish/pallas_call | solution.py:130
  (10 shorter events, 0.2 us)
Async XLA Ops:
  0.6 16.4 %all-to-all-start = ((f32[8,128,128]{2,1,0:T(8,128)}), f32[8,128,128]{2,1,0:T(8,128)S(1)}, u32[]{:S(2)}, u32[]{:S(2)}) async-start(f32[8,128,128]{2,1,0:T(8,128)} %bitcast.38), calls=%async_computation | async-start | bytes 1048576 | tf_op jit(solution)/shard_map/all_to_all | solution.py:101
  11.5 8.8 %collective-permute-start.2 = (f32[64,128]{1,0:T(8,128)S(1)}, f32[64,128]{1,0:T(8,128)S(1)}, u32[]{:S(2)}, u32[]{:S(2)}) collective-permute-start(f32[64,128]{1,0:T(8,128)S(1)} %bitcast.34), channel_id=1, source_target_pairs={{0,64},{32,96},{64,0},{96,32},{128,192},{160,224},{192,128},{224,1... | collective-permute-start | bytes 98312 | tf_op jit(solution)/shard_map/ppermute | solution.py:100
  17.1 7.8 %collective-permute-start = (f32[128,128]{1,0:T(8,128)S(1)}, f32[128,128]{1,0:T(8,128)S(1)}, u32[]{:S(2)}, u32[]{:S(2)}) collective-permute-start(f32[128,128]{1,0:T(8,128)S(1)} %multiply_reduce_fusion), channel_id=1, source_target_pairs={{0,64},{32,96},{64,0},{96,32},{128,192},{160,224},{192,128},{224,1... | collective-permute-start | bytes 196616 | tf_op jit(solution)/shard_map/ppermute | solution.py:106
  20.4 15.8 %collective-permute-start.3 = (f32[128,128]{1,0:T(8,128)S(1)}, f32[128,128]{1,0:T(8,128)S(1)}, u32[]{:S(2)}, u32[]{:S(2)}) collective-permute-start(f32[128,128]{1,0:T(8,128)S(1)} %bitcast.40), channel_id=1, source_target_pairs={{0,32},{32,0},{64,96},{96,64},{128,160},{160,128},{192,224},{224,1... | collective-permute-start | bytes 196616 | tf_op jit(solution)/shard_map/ppermute | solution.py:110
  25.6 14.1 %all-to-all-start.1 = ((f32[64,1,128]{2,1,0:T(1,128)}), f32[64,1,128]{2,1,0:T(1,128)S(1)}, u32[]{:S(2)}, u32[]{:S(2)}) async-start(f32[64,1,128]{2,1,0:T(1,128)} %broadcast_in_dim.7), calls=%async_computation.1 | async-start | bytes 65536 | tf_op jit(solution)/shard_map/all_to_all | solution.py:115
  32.7 7.0 %collective-permute-start.1 = (f32[128,128]{1,0:T(8,128)S(1)}, f32[128,128]{1,0:T(8,128)S(1)}, u32[]{:S(2)}, u32[]{:S(2)}) collective-permute-start(f32[128,128]{1,0:T(8,128)S(1)} %get-tuple-element.17), channel_id=1, source_target_pairs={{0,32},{32,0},{64,96},{96,64},{128,160},{160,128},{192,224},{224,1... | collective-permute-start | bytes 196616 | tf_op jit(solution)/shard_map/ppermute | solution.py:114
  39.7 24.8 %copy-start = (f32[131072]{0:T(1024)S(1)}, f32[131072]{0:T(1024)}, u32[]{:S(2)}) copy-start(f32[131072]{0:T(1024)} %param.5) | copy-start | bytes 1572868
  40.8 23.6 %all-to-all-start.2 = ((f32[4,2,256,128]{3,2,1,0:T(8,128)}), f32[4,2,256,128]{3,2,1,0:T(8,128)S(1)}, u32[]{:S(2)}, u32[]{:S(2)}) async-start(f32[4,2,256,128]{3,2,1,0:T(8,128)} %broadcast_in_dim.8), calls=%async_computation.2 | async-start | bytes 2097152 | tf_op jit(solution)/shard_map/all_to_all | solution.py:124
